TPU v7x, 128 devices: a whole 4x4x4 slice. The times are simulated.
128 devices in a mesh: rows: 8 (over y, core), cols: 16 (over z, x).
Axes of the slice: x: 4, y: 4, z: 4, core: 2. Of those that a mesh axis runs over, the one named last changes fastest.
Arguments:
- state: float32 [8, 256, 512, 512], P(None, 'rows', 'cols'), may hold values from -4 to 10, as said below
- flags: int32 [16, 32, 32], P('rows', 'cols'), may hold values from 0 to 1, as said below
- owners: int32 [2048, 1], P(('rows', 'cols')), may hold values from 0 to 15; in each aligned block of 16 rows (0 to 15, 16 to 31, ...) at most 2 rows name the same one
Outputs:
- faces_new: float32 [3, 256, 512, 512], P(None, 'rows', 'cols')
- arrivals: float32 [8, 16, 16, 2, 8, 4096], P('rows', 'cols')
Inputs may be any that keep to these rules, and one draw needn't show every extreme that they name: `state`: density (field 0) is positive, energy (field 1) lies in 1 to 10. `flags`: each device's 2 x 2 x 32 meshblocks hold exactly 2 flagged ones. `owners`: among the 16 rows of one device, no column is named more than 2 times.
All inputs are finite; a program needn't handle non-finite values.
Results may differ from a plain program's by a relative error of at most 0.0003.
Values sent between devices are 32-bit elements; how exact they have to be, the bound alone decides.
No kernel may reach another device: no remote copies, remote signals or barrier semaphores. Data moves between devices by JAX's collectives and lax.ppermute only.
A program may use at most 320 MiB of HBM per device.

v0:
```python
import jax
import jax.numpy as jnp
from jax import lax
from jax.sharding import PartitionSpec as P

BS = 16
CAP = 2


courant = 0.3


def with_halo(array, sides, width):
    for axis, dim in sides:
        count, length = (lax.axis_size(axis), array.shape[dim])
        up = [(i, (i + 1) % count) for i in range(count - 1)]
        down = [(j, i) for i, j in up]
        last = lax.slice_in_dim(array, length - width, length, axis=dim)
        leading = lax.slice_in_dim(array, 0, width, axis=dim)
        before = lax.ppermute(last, axis, up)
        after = lax.ppermute(leading, axis, down)
        array = jnp.concatenate([before, array, after], axis=dim)
    return array


def minmod(left, right):
    return jnp.maximum(jnp.minimum(left, right), 0.0) + jnp.minimum(jnp.maximum(left, right), 0.0)


def upper_next(values):
    widths = ((0, 0),) * (values.ndim - 1) + ((0, 1),)
    return jnp.pad(values[..., 1:], widths)


def lower_next(values):
    widths = ((0, 0),) * (values.ndim - 1) + ((1, 0),)
    return jnp.pad(values[..., :-1], widths)


def advance_core(core, face_x_next, face_y_next, row_at, col_at, row_count, col_count):
    span_x = core.shape[1]
    span_y = core.shape[2]
    place_x = jnp.arange(span_x)
    place_y = jnp.arange(span_y)
    outer_x = (row_at == 0) & (place_x < 1) | (row_at == row_count - 1) & (place_x >= span_x - 1)
    outer_y = (col_at == 0) & (place_y < 1) | (col_at == col_count - 1) & (place_y >= span_y - 1)
    outside = outer_x[:, None, None] | outer_y[None, :, None]
    density = jnp.where(outside, 1.0, core[0])
    velocity = core[2:5] / density
    field_x = 0.5 * (core[5] + face_x_next)
    field_y = 0.5 * (core[6] + face_y_next)
    field_z = 0.5 * (core[7] + upper_next(core[7]))
    elec_x = velocity[2] * field_y - velocity[1] * field_z
    elec_y = velocity[0] * field_z - velocity[2] * field_x
    elec_z = velocity[1] * field_x - velocity[0] * field_y
    edge_z = 0.25 * (elec_z[:-1, :-1] + elec_z[:-1, 1:] + elec_z[1:, :-1] + elec_z[1:, 1:])
    lower_y = elec_y[:-1, 1:-1]
    higher_y = elec_y[1:, 1:-1]
    edge_y_low = 0.25 * (lower_next(lower_y) + lower_y + lower_next(higher_y) + higher_y)
    edge_y_high = 0.25 * (lower_y + upper_next(lower_y) + higher_y + upper_next(higher_y))
    lower_x = elec_x[1:-1, :-1]
    higher_x = elec_x[1:-1, 1:]
    edge_x_low = 0.25 * (lower_next(lower_x) + lower_x + lower_next(higher_x) + higher_x)
    edge_x_high = 0.25 * (lower_x + upper_next(lower_x) + higher_x + upper_next(higher_x))
    face_vals = core[5:8, 1:-1, 1:-1]
    new_x = face_vals[0] - courant * (
        edge_z[:-1, 1:] - edge_z[:-1, :-1] - (edge_y_high[:-1] - edge_y_low[:-1])
    )
    new_y = face_vals[1] - courant * (
        edge_x_high[:, :-1] - edge_x_low[:, :-1] - (edge_z[1:, :-1] - edge_z[:-1, :-1])
    )
    new_z = face_vals[2] - courant * (
        edge_y_low[1:] - edge_y_low[:-1] - (edge_x_low[:, 1:] - edge_x_low[:, :-1])
    )
    return jnp.stack([new_x, new_y, new_z], axis=0)


def prolong(coarse_piece):
    half_cells = coarse_piece.shape[1] - 2
    centre = coarse_piece[:5, 1:-1, 1:-1, 1:-1]
    slope_x = minmod(
        coarse_piece[:5, 2:, 1:-1, 1:-1] - centre, centre - coarse_piece[:5, :-2, 1:-1, 1:-1]
    )
    slope_y = minmod(
        coarse_piece[:5, 1:-1, 2:, 1:-1] - centre, centre - coarse_piece[:5, 1:-1, :-2, 1:-1]
    )
    slope_z = minmod(
        coarse_piece[:5, 1:-1, 1:-1, 2:] - centre, centre - coarse_piece[:5, 1:-1, 1:-1, :-2]
    )
    offsets = jnp.array([-0.25, 0.25], jnp.float32)
    fine_cells = (
        centre[:, :, None, :, None, :, None]
        + offsets.reshape(1, 1, 2, 1, 1, 1, 1) * slope_x[:, :, None, :, None, :, None]
        + offsets.reshape(1, 1, 1, 1, 2, 1, 1) * slope_y[:, :, None, :, None, :, None]
        + offsets.reshape(1, 1, 1, 1, 1, 1, 2) * slope_z[:, :, None, :, None, :, None]
    )
    fine_cells = fine_cells.reshape(5, -1)
    fine_shape = (half_cells, 2, half_cells, 2, half_cells, 2)
    face_x = coarse_piece[5, 1:, 1:-1, 1:-1]
    fine_x = jnp.stack([face_x[:-1], 0.5 * (face_x[:-1] + face_x[1:])], axis=1)[
        :, :, :, None, :, None
    ]
    face_y = coarse_piece[6, 1:-1, 1:, 1:-1]
    fine_y = jnp.stack([face_y[:, :-1], 0.5 * (face_y[:, :-1] + face_y[:, 1:])], axis=2)[
        :, None, :, :, :, None
    ]
    face_z = coarse_piece[7, 1:-1, 1:-1, 1:]
    fine_z = jnp.stack([face_z[:, :, :-1], 0.5 * (face_z[:, :, :-1] + face_z[:, :, 1:])], axis=3)[
        :, None, :, None, :, :
    ]
    fine_faces = jnp.stack(
        [
            jnp.broadcast_to(fine_x, fine_shape),
            jnp.broadcast_to(fine_y, fine_shape),
            jnp.broadcast_to(fine_z, fine_shape),
        ],
        axis=0,
    ).reshape(3, -1)
    return jnp.concatenate([fine_cells, fine_faces], axis=0)


def child_slots(flag_list, owner_list, column_count):
    block_count = flag_list.shape[0]
    parent_count = owner_list.shape[0] // 8
    running = jnp.cumsum(flag_list)
    rank_ids = jnp.arange(parent_count, dtype=jnp.int32)
    matches = (flag_list[None, :] == 1) & (running[None, :] == rank_ids[:, None] + 1)
    position = jnp.sum(
        jnp.where(matches, jnp.arange(block_count, dtype=jnp.int32)[None, :], 0), axis=1
    )
    onehot = (owner_list[:, None] == jnp.arange(column_count, dtype=jnp.int32)[None, :]).astype(
        jnp.int32
    )
    earlier = jnp.cumsum(onehot, axis=0) - onehot
    order_rank = jnp.sum(earlier * onehot, axis=1)
    return (position, owner_list * CAP + order_rank)


def piece_starts(position, blocks_y, blocks_z):
    child_ids = jnp.arange(position.shape[0] * 8, dtype=jnp.int32)
    parent_pos = position[child_ids // 8]
    octant = child_ids % 8
    half_cells = BS // 2
    start_x = BS * (parent_pos // (blocks_y * blocks_z)) + half_cells * (octant // 4)
    start_y = BS * (parent_pos // blocks_z % blocks_y) + half_cells * (octant // 2 % 2)
    start_z = BS * (parent_pos % blocks_z) + half_cells * (octant % 2) - 1
    return (start_x, start_y, start_z)


def cut_pieces(core, start_x, start_y, start_z, row_at, col_at, row_count, col_count):
    piece_span = BS // 2 + 2
    span_x = core.shape[1]
    span_y = core.shape[2]
    width_z = core.shape[3]
    steps_along = jnp.arange(piece_span, dtype=jnp.int32)
    density_field = (jnp.arange(8, dtype=jnp.int32) == 0)[:, None, None, None]

    def one_piece(corner_x, corner_y, corner_z):
        anchor = jnp.zeros((), jnp.int32)
        window_z = jnp.clip(corner_z, 0, width_z - piece_span)
        window = lax.dynamic_slice(
            core, (anchor, corner_x, corner_y, window_z), (8, piece_span, piece_span, piece_span)
        )
        pick = jnp.clip(corner_z + steps_along - window_z, 0, piece_span - 1)
        window = jnp.take(window, pick, axis=3)
        place_x = corner_x + steps_along
        place_y = corner_y + steps_along
        place_z = corner_z + steps_along
        outer_x = (row_at == 0) & (place_x < 1) | (row_at == row_count - 1) & (
            place_x >= span_x - 1
        )
        outer_y = (col_at == 0) & (place_y < 1) | (col_at == col_count - 1) & (
            place_y >= span_y - 1
        )
        outer_z = (place_z < 0) | (place_z >= width_z)
        outside = outer_x[:, None, None] | outer_y[None, :, None] | outer_z[None, None, :]
        filler = jnp.where(density_field, 1.0, 0.0)
        return jnp.where(outside[None], filler, window)

    return jax.vmap(one_piece)(start_x, start_y, start_z)


def on_device(state, flags, owners):
    row_at = lax.axis_index("rows")
    col_at = lax.axis_index("cols")
    row_count = lax.axis_size("rows")
    column_count = lax.axis_size("cols")
    extended = with_halo(state, (("rows", 1), ("cols", 2)), 2)
    core = extended[:, 1:-1, 1:-1]
    face_x_next = extended[5, 2:, 1:-1]
    face_y_next = extended[6, 1:-1, 2:]
    faces_new = advance_core(
        core, face_x_next, face_y_next, row_at, col_at, row_count, column_count
    )
    position, slot_index = child_slots(flags.reshape(-1), owners[:, 0], column_count)
    start_x, start_y, start_z = piece_starts(position, flags.shape[1], flags.shape[2])
    pieces = cut_pieces(core, start_x, start_y, start_z, row_at, col_at, row_count, column_count)
    children = jax.vmap(prolong)(pieces)
    buffer = (
        jnp.zeros((column_count * CAP,) + children.shape[1:], jnp.float32)
        .at[slot_index]
        .set(children)
    )
    arrivals = lax.all_to_all(
        buffer.reshape((column_count, CAP) + children.shape[1:]),
        "cols",
        split_axis=0,
        concat_axis=0,
        tiled=True,
    )
    return (faces_new, arrivals[None, None])


def solution(mesh):
    return jax.shard_map(
        on_device,
        mesh=mesh,
        in_specs=(
            P(None, "rows", "cols", None),
            P("rows", "cols", None),
            P(("rows", "cols"), None),
        ),
        out_specs=(P(None, "rows", "cols", None), P("rows", "cols", None, None, None, None)),
        check_vma=False,
    )
```

profile of v0, /device:TPU:8, one launch (start us, length us, event | category | flops | bytes accessed | tf_op | source)
XLA Modules:
  0.0 353.0 jit_solution(7166455176688743847)
XLA Ops:
  12.1 7.7 %collective-permute-done = f32[8,2,32,512]{3,2,1,0:T(8,128)S(1)} collective-permute-done((f32[8,2,32,512]{3,2,1,0:T(8,128)}, f32[8,2,32,512]{3,2,1,0:T(8,128)S(1)}, u32[]{:S(2)}, u32[]{:S(2)}) %collective-permute-start) | collective-permute-done | bytes 1048608 | tf_op jit(solution)/shard_map/ppermute | solution.py:20
  19.8 8.0 %constant_dynamic-update-slice_fusion.2 = f32[8,36,32,512]{3,2,1,0:T(8,128)S(1)} fusion(f32[8,36,32,512]{3,2,1,0:T(8,128)S(1)} %constant_dynamic-update-slice_fusion.3, f32[8,32,32,512]{3,2,1,0:T(8,128)} %param.4), kind=kLoop, calls=%fused_computation.101 | loop fusion | bytes 33554432
  28.0 6.5 %copy-done = f32[8,36,32,512]{3,2,1,0:T(8,128)} copy-done((f32[8,36,32,512]{3,2,1,0:T(8,128)}, f32[8,36,32,512]{3,2,1,0:T(8,128)S(1)}, u32[]{:S(2)}) %copy-start) | copy-done | bytes 18874392
  38.3 4.8 %collective-permute-start.2 = (f32[8,36,2,512]{3,2,1,0:T(2,128)}, f32[8,36,2,512]{3,2,1,0:T(2,128)S(1)}, u32[]{:S(2)}, u32[]{:S(2)}) collective-permute-start(f32[8,36,2,512]{3,2,1,0:T(2,128)} %get-tuple-element.32), channel_id=1, source_target_pairs={{0,1},{1,2},{2,3},{3,4},{4,5},{5,6},{6,7},{7,8},{8,9},{9,10},{10,1... | collective-permute-start | bytes 3538952 | tf_op jit(solution)/shard_map/ppermute | solution.py:20
  44.2 22.1 %collective-permute-done.3 = f32[8,36,2,512]{3,2,1,0:T(2,128)S(1)} collective-permute-done((f32[8,36,2,512]{3,2,1,0:T(2,128)}, f32[8,36,2,512]{3,2,1,0:T(2,128)S(1)}, u32[]{:S(2)}, u32[]{:S(2)}) %collective-permute-start.3) | collective-permute-done | bytes 1179680 | tf_op jit(solution)/shard_map/ppermute | solution.py:21
  67.6 9.2 %pad_maximum_fusion = f32[8,36,36,512]{3,2,1,0:T(8,128)S(1)} fusion(f32[8,36,2,512]{3,2,1,0:T(2,128)S(1)} %collective-permute-done.3, f32[8,36,32,512]{3,2,1,0:T(8,128)} %copy-done, f32[8,36,2,512]{3,2,1,0:T(2,128)S(1)} %collective-permute-done.2), kind=kLoop, calls=%fused_computation.5 | loop fusion | flops 10616832 | bytes 42467328 | tf_op jit(solution)/shard_map/concatenate | solution.py:22
  76.8 11.2 %slice.332 = f32[8,34,34,512]{3,2,1,0:T(8,128)} slice(f32[8,36,36,512]{3,2,1,0:T(8,128)S(1)} %pad_maximum_fusion), slice={[0:8], [1:35], [1:35], [0:512]} | slice | bytes 37879808 | tf_op jit(solution)/shard_map/slice | solution.py:189
  91.3 91.2 %while.1 = (s32[]{:T(128)}, f32[8,34,34,512]{3,2,1,0:T(8,128)}, s32[16,4]{0,1:T(4,128)S(1)}, f32[16,8,10,10,10]{3,1,4,2,0:T(8,128)}, s32[]{:T(128)}) while((s32[]{:T(128)}, f32[8,34,34,512]{3,2,1,0:T(8,128)}, s32[16,4]{0,1:T(4,128)S(1)}, f32[16,8,10,10,10]{3,1,4,2,0:T(8,128)}, s32[]{:T(128)}) %tuple.56), condition=%wide.while_cond, body=%wide.while_body.sunk | while | flops 2 | bytes 569745 | solution.py:161
  91.9 3.8 %dynamic-slice_bitcast_fusion.2 = f32[1,8,10,10,10]{4,3,2,1,0:T(8,128)S(1)} fusion(f32[8,34,34,512]{3,2,1,0:T(8,128)} %get-tuple-element.115, s32[]{:T(128)} %bitcast.115, s32[]{:T(128)} %bitcast.116, s32[]{:T(128)} %bitcast.117), kind=kLoop, calls=%fused_computation.2.clone.1 | loop fusion | bytes 64012 | tf_op jit(solution)/shard_map/vmap()/gather
  97.7 3.8 %dynamic-slice_bitcast_fusion.2 = f32[1,8,10,10,10]{4,3,2,1,0:T(8,128)S(1)} fusion(f32[8,34,34,512]{3,2,1,0:T(8,128)} %get-tuple-element.115, s32[]{:T(128)} %bitcast.115, s32[]{:T(128)} %bitcast.116, s32[]{:T(128)} %bitcast.117), kind=kLoop, calls=%fused_computation.2.clone.1 | loop fusion | bytes 64012 | tf_op jit(solution)/shard_map/vmap()/gather
  103.4 3.8 %dynamic-slice_bitcast_fusion.2 = f32[1,8,10,10,10]{4,3,2,1,0:T(8,128)S(1)} fusion(f32[8,34,34,512]{3,2,1,0:T(8,128)} %get-tuple-element.115, s32[]{:T(128)} %bitcast.115, s32[]{:T(128)} %bitcast.116, s32[]{:T(128)} %bitcast.117), kind=kLoop, calls=%fused_computation.2.clone.1 | loop fusion | bytes 64012 | tf_op jit(solution)/shard_map/vmap()/gather
  166.4 3.8 %dynamic-slice_bitcast_fusion.2 = f32[1,8,10,10,10]{4,3,2,1,0:T(8,128)S(1)} fusion(f32[8,34,34,512]{3,2,1,0:T(8,128)} %get-tuple-element.115, s32[]{:T(128)} %bitcast.115, s32[]{:T(128)} %bitcast.116, s32[]{:T(128)} %bitcast.117), kind=kLoop, calls=%fused_computation.2.clone.1 | loop fusion | bytes 64012 | tf_op jit(solution)/shard_map/vmap()/gather
  182.5 7.4 %gather_fusion = f32[160,8,10,10]{3,1,2,0:T(8,128)} fusion(f32[16,8,10,10,10]{3,1,4,2,0:T(8,128)} %get-tuple-element.9, s32[160]{0:T(256)S(1)} %reshape.781), kind=kCustom, calls=%fused_computation | custom fusion | bytes 1025280 | tf_op jit(solution)/shard_map/vmap(jit(_take))/gather | solution.py:165
  189.9 10.9 %copy.70 = f32[16,10,8,10,10]{0,1,4,3,2:T(8,128)} copy(f32[16,10,8,10,10]{4,2,3,1,0:T(8,128)} %bitcast.118) | data formatting | bytes 1024000 | tf_op jit(solution)/shard_map/vmap(jit(_take))/gather | solution.py:165
  200.8 3.8 %bitcast_select_fusion = f32[16,8,10,10,10]{0,4,3,2,1:T(8,128)S(1)} fusion(f32[16,10,8,10,10]{0,1,4,3,2:T(8,128)} %copy.70, f32[8]{0:T(128)S(1)} %compare_select_fusion.16, pred[16,10]{0,1:T(8,128)(4,1)S(1)} %get-tuple-element.64, pred[16,10,10,10]{0,3,2,1:T(8,128)(4,1)S(1)} %copy-done.8), kind=kLoop, calls=%fused_computation.7 | loop fusion | flops 256000 | bytes 1040192 | tf_op jit(solution)/shard_map/vmap(jit(_where))/select_n | solution.py:178
  207.6 4.4 %maximum_bitcast_fusion = (f32[34,34,512]{2,1,0:T(8,128)S(1)}, f32[34,34,512]{2,1,0:T(8,128)S(1)}) fusion(f32[8,36,2,512]{3,2,1,0:T(2,128)S(1)} %collective-permute-done.3, f32[8,36,32,512]{3,2,1,0:T(8,128)} %copy-done, f32[8,36,2,512]{3,2,1,0:T(2,128)S(1)} %collective-permute-done.2, pred[34,34]{1,0:T(8,128)(4,1)S(1)} %broadcast_or_fusion.2), kind=kLoop, calls=%fused_computation.12 | loop fusion | flops 2959360 | bytes 25969796 | tf_op jit(solution)/shard_map/squeeze | solution.py:52
  212.1 10.0 %slice_divide_fusion = f32[3,34,34,512]{3,2,1,0:T(8,128)} fusion(f32[8,36,36,512]{3,2,1,0:T(8,128)} %copy-done.1, f32[34,34,512]{2,1,0:T(8,128)S(1)} %get-tuple-element.29), kind=kLoop, calls=%fused_computation.6 | loop fusion | flops 1775616 | bytes 16572416 | tf_op jit(solution)/shard_map/div | solution.py:49
  229.0 8.2 %pad_maximum_fusion.2 = f32[3,16,8,2,8,2,8,2]{1,7,6,5,4,3,2,0:T(2,128)} fusion(f32[1,16,8,2,8,2,8,2]{1,7,6,5,4,3,2,0:T(2,128)S(1)} %broadcast_in_dim.81, f32[1,16,8,2,8,2,8,2]{1,7,6,5,4,3,2,0:T(2,128)S(1)} %broadcast_in_dim.80, f32[1,16,8,2,8,2,8,2]{1,7,6,5,4,3,2,0:T(2,128)} %broadcast_in_dim.79), kind=kLoop, calls=%fused_computation.9 | loop fusion | flops 393216 | bytes 1572864 | tf_op jit(solution)/shard_map/vmap()/stack | solution.py:111
  237.2 4.8 %copy.75 = f32[16,3,4096]{2,1,0:T(4,128)S(1)} copy(f32[16,3,4096]{0,2,1:T(8,128)} %bitcast.121) | data formatting | bytes 1572864 | tf_op jit(solution)/shard_map/vmap()/reshape | solution.py:118
  248.0 8.8 %broadcast_add_fusion = f32[16,5,8,2,8,2,8,2]{0,7,6,5,4,3,2,1:T(2,128)} fusion(f32[16,5,8,8,8,2]{0,5,4,3,2,1:T(2,128)S(1)} %broadcast_multiply_fusion, f32[16,5,8,2,8,2,8]{0,6,5,4,3,2,1:T(8,128)S(1)} %broadcast_add_fusion.1), kind=kLoop, calls=%fused_computation.10 | loop fusion | flops 327680 | bytes 2293760 | tf_op jit(solution)/shard_map/vmap()/add | solution.py:92
  256.7 8.2 %copy.74 = f32[16,5,4096]{2,1,0:T(8,128)} copy(f32[16,5,4096]{0,2,1:T(8,128)} %bitcast.119) | data formatting | bytes 2621440 | tf_op jit(solution)/shard_map/vmap()/add | solution.py:92
  270.8 4.4 %scatter_fusion = f32[32,8,4096]{2,1,0:T(8,128)} fusion(f32[32,8,4096]{2,1,0:T(8,128)} %broadcast_in_dim.70, s32[16]{0:T(128)S(1)} %fusion.66, f32[16,8,4096]{2,1,0:T(8,128)} %pad_maximum_fusion.4), kind=kCustom, calls=%fused_computation.1 | custom fusion | bytes 6291520 | tf_op jit(solution)/shard_map/scatter | solution.py:202
  275.2 9.6 %all-to-all-start = ((f32[16,2,8,4096]{3,2,1,0:T(8,128)}), f32[16,2,8,4096]{3,2,1,0:T(8,128)}, u32[]{:S(2)}, u32[]{:S(2)}) async-start(f32[16,2,8,4096]{3,2,1,0:T(8,128)} %bitcast.120), calls=%async_computation | async-start | bytes 8388608 | tf_op jit(solution)/shard_map/all_to_all | solution.py:204
  284.8 11.3 %multiply_subtract_fusion.2 = (f32[34,34,512]{2,1,0:T(8,128)}, f32[34,34,512]{2,1,0:T(8,128)}, f32[34,34,512]{2,1,0:T(8,128)}) fusion(f32[3,34,34,512]{3,2,1,0:T(8,128)} %slice_divide_fusion, f32[8,36,2,512]{3,2,1,0:T(2,128)S(1)} %collective-permute-done.3, f32[8,36,32,512]{3,2,1,0:T(8,128)} %copy-done, f32[8,36,2,512]{3,2,1,0:T(2,128)S(1)} %collective-permute-done.2), kind=kLoop, calls=%fused_computation.27 | loop fusion | flops 8286208 | bytes 33071104 | tf_op jit(solution)/shard_map/sub | solution.py:55
  296.1 9.1 %multiply_subtract_fusion.1 = (f32[34,34,512]{2,1,0:T(8,128)S(1)}, f32[34,34,512]{2,1,0:T(8,128)S(1)}) fusion(f32[34,34,512]{2,1,0:T(8,128)} %get-tuple-element.23, f32[3,34,34,512]{3,2,1,0:T(8,128)} %slice_divide_fusion, f32[34,34,512]{2,1,0:T(8,128)} %copy-done.2, f32[34,34,511]{2,1,0:T(8,128)} %slice.309, f32[34,34,512]{2,1,0:T(8,128)} %get-tuple-element.24), kind=kLoop, calls=%fused_computation.25 | loop fusion | flops 4734976 | bytes 21302768 | tf_op jit(solution)/shard_map/sub | solution.py:54
  305.2 5.8 %fusion.6 = f32[33,33,512]{2,1,0:T(8,128)S(1)} fusion(f32[34,34,512]{2,1,0:T(8,128)} %get-tuple-element.22), kind=kLoop, calls=%fused_computation.29 | loop fusion | flops 2230272 | bytes 11151360 | tf_op jit(solution)/shard_map/mul | solution.py:56
  317.7 4.2 %fusion.78 = (f32[32,33,511]{2,1,0:T(8,128)S(1)}, f32[32,33,511]{2,1,0:T(8,128)}, f32[32,33,511]{2,1,0:T(8,128)}, f32[32,33,511]{2,1,0:T(8,128)S(1)}) fusion(f32[34,34,512]{2,1,0:T(8,128)S(1)} %get-tuple-element.37), kind=kLoop, calls=%fused_computation.222 | loop fusion | bytes 17267712 | tf_op jit(solution)/shard_map/slice | solution.py:32
  321.9 6.7 %fusion.77 = (f32[32,33,512]{2,1,0:T(8,128)}, f32[32,33,512]{2,1,0:T(8,128)S(1)}, f32[32,33,512]{2,1,0:T(8,128)}) fusion(f32[34,34,512]{2,1,0:T(8,128)S(1)} %get-tuple-element.37, f32[32,33,511]{2,1,0:T(8,128)} %get-tuple-element.53, f32[32,33,511]{2,1,0:T(8,128)} %get-tuple-element.54), kind=kLoop, calls=%fused_computation.221 | loop fusion | flops 2162688 | bytes 15130368 | tf_op jit(solution)/shard_map/slice | solution.py:61
  328.7 3.9 %fusion.10 = f32[1,32,32,512]{3,2,1,0:T(8,128)} fusion(f32[32,33,512]{2,1,0:T(8,128)S(1)} %get-tuple-element.50, f32[33,32,512]{2,1,0:T(8,128)S(1)} %get-tuple-element.43, f32[8,32,32,512]{3,2,1,0:T(8,128)} %param.4), kind=kLoop, calls=%fused_computation.40 | loop fusion | flops 2621440 | bytes 12582912 | tf_op jit(solution)/shard_map/stack | solution.py:75
  332.6 8.6 %fusion.22 = (f32[1,32,32,512]{3,2,1,0:T(8,128)}, f32[1,32,32,512]{3,2,1,0:T(8,128)}) fusion(f32[33,32,511]{2,1,0:T(8,128)S(1)} %copy-done.4, f32[33,32,512]{2,1,0:T(8,128)} %get-tuple-element.44, f32[33,32,511]{2,1,0:T(8,128)S(1)} %copy-done.3, f32[33,32,512]{2,1,0:T(8,128)} %get-tuple-element.42, f32[33,33,512]{2,1,0:T(8,128)S(1)} %fusion.6, ...), kind=kLoop, calls=%fused_computation.58 | loop fusion | flops 9437184 | bytes 35896832 | tf_op jit(solution)/shard_map/stack | solution.py:75
  341.2 6.9 %pad_maximum_fusion.1 = f32[3,32,32,512]{3,2,1,0:T(8,128)} fusion(f32[1,32,32,512]{3,2,1,0:T(8,128)} %fusion.10, f32[1,32,32,512]{3,2,1,0:T(8,128)} %get-tuple-element.31, f32[1,32,32,512]{3,2,1,0:T(8,128)} %get-tuple-element.30), kind=kLoop, calls=%fused_computation.8 | loop fusion | flops 3145728 | bytes 12582912 | tf_op jit(solution)/shard_map/stack | solution.py:75
  348.1 4.7 %copy.103 = f32[1,1,16,2,8,4096]{5,4,3,2,1,0:T(8,128)} copy(f32[1,1,16,2,8,4096]{5,4,3,2,1,0:T(8,128)} %bitcast.34) | data formatting | bytes 8388608
  (161 shorter events, 125.4 us)
Async XLA Ops:
  0.6 8.4 %copy-start.9 = (s32[2,2,32]{2,1,0:T(2,128)S(1)}, s32[2,2,32]{2,1,0:T(2,128)}, u32[]{:S(2)}) copy-start(s32[2,2,32]{2,1,0:T(2,128)} %param.5) | copy-start | bytes 1540
  0.6 8.5 %copy-start.11 = (s32[16,1]{0,1:T(1,128)S(1)}, s32[16,1]{0,1:T(1,128)}, u32[]{:S(2)}) copy-start(s32[16,1]{0,1:T(1,128)} %param.6) | copy-start | bytes 196
  3.4 16.3 %collective-permute-start = (f32[8,2,32,512]{3,2,1,0:T(8,128)}, f32[8,2,32,512]{3,2,1,0:T(8,128)S(1)}, u32[]{:S(2)}, u32[]{:S(2)}) collective-permute-start(f32[8,2,32,512]{3,2,1,0:T(8,128)} %get-tuple-element.35), channel_id=1, source_target_pairs={{0,16},{16,32},{32,48},{48,64},{64,80},{80,96},{96,112},{1,17},{17... | collective-permute-start | bytes 3145736 | tf_op jit(solution)/shard_map/ppermute | solution.py:20
  5.3 22.5 %collective-permute-start.1 = (f32[8,2,32,512]{3,2,1,0:T(8,128)S(1)}, f32[8,2,32,512]{3,2,1,0:T(8,128)S(1)}, u32[]{:S(2)}, u32[]{:S(2)}) collective-permute-start(f32[8,2,32,512]{3,2,1,0:T(8,128)S(1)} %get-tuple-element.34), channel_id=1, source_target_pairs={{16,0},{32,16},{48,32},{64,48},{80,64},{96,80},{112,96},{17,1},{33... | collective-permute-start | bytes 3145736 | tf_op jit(solution)/shard_map/ppermute | solution.py:21
  28.0 6.5 %copy-start = (f32[8,36,32,512]{3,2,1,0:T(8,128)}, f32[8,36,32,512]{3,2,1,0:T(8,128)S(1)}, u32[]{:S(2)}) copy-start(f32[8,36,32,512]{3,2,1,0:T(8,128)S(1)} %constant_dynamic-update-slice_fusion.1) | copy-start | bytes 56623108
  37.0 29.3 %collective-permute-start.3 = (f32[8,36,2,512]{3,2,1,0:T(2,128)}, f32[8,36,2,512]{3,2,1,0:T(2,128)S(1)}, u32[]{:S(2)}, u32[]{:S(2)}) collective-permute-start(f32[8,36,2,512]{3,2,1,0:T(2,128)} %get-tuple-element.33), channel_id=1, source_target_pairs={{1,0},{2,1},{3,2},{4,3},{5,4},{6,5},{7,6},{8,7},{9,8},{10,9},{11,1... | collective-permute-start | bytes 3538952 | tf_op jit(solution)/shard_map/ppermute | solution.py:21
  38.3 29.3 %collective-permute-start.2 = (f32[8,36,2,512]{3,2,1,0:T(2,128)}, f32[8,36,2,512]{3,2,1,0:T(2,128)S(1)}, u32[]{:S(2)}, u32[]{:S(2)}) collective-permute-start(f32[8,36,2,512]{3,2,1,0:T(2,128)} %get-tuple-element.32), channel_id=1, source_target_pairs={{0,1},{1,2},{2,3},{3,4},{4,5},{5,6},{6,7},{7,8},{8,9},{9,10},{10,1... | collective-permute-start | bytes 3538952 | tf_op jit(solution)/shard_map/ppermute | solution.py:20
  76.8 14.5 %copy-start.1 = (f32[8,36,36,512]{3,2,1,0:T(8,128)}, f32[8,36,36,512]{3,2,1,0:T(8,128)S(1)}, u32[]{:S(2)}) copy-start(f32[8,36,36,512]{3,2,1,0:T(8,128)S(1)} %pad_maximum_fusion) | copy-start | bytes 63700996
  189.9 10.9 %copy-start.8 = (pred[16,10,10,10]{0,3,2,1:T(8,128)(4,1)S(1)}, pred[16,10,10,10]{0,3,2,1:T(8,128)(4,1)}, u32[]{:S(2)}) copy-start(pred[16,10,10,10]{0,3,2,1:T(8,128)(4,1)} %broadcast_or_fusion) | copy-start | bytes 48004
  212.1 10.0 %copy-start.2 = (f32[34,34,512]{2,1,0:T(8,128)}, f32[34,34,512]{2,1,0:T(8,128)S(1)}, u32[]{:S(2)}) copy-start(f32[34,34,512]{2,1,0:T(8,128)S(1)} %get-tuple-element.28) | copy-start | bytes 7102468
  237.2 4.9 %copy-start.10 = (f32[2]{0:T(128)S(1)}, f32[2]{0:T(128)}, u32[]{:S(2)}) copy-start(f32[2]{0:T(128)} %constant.178.clone) | copy-start | bytes 28
  242.1 2.7 copy-start.5
  244.8 1.3 copy-start.6
  244.8 1.7 copy-start.7
  275.2 72.9 %all-to-all-start = ((f32[16,2,8,4096]{3,2,1,0:T(8,128)}), f32[16,2,8,4096]{3,2,1,0:T(8,128)}, u32[]{:S(2)}, u32[]{:S(2)}) async-start(f32[16,2,8,4096]{3,2,1,0:T(8,128)} %bitcast.120), calls=%async_computation | async-start | bytes 8388608 | tf_op jit(solution)/shard_map/all_to_all | solution.py:204
  328.7 3.9 %copy-start.3 = (f32[33,32,511]{2,1,0:T(8,128)S(1)}, f32[33,32,511]{2,1,0:T(8,128)}, u32[]{:S(2)}) copy-start(f32[33,32,511]{2,1,0:T(8,128)} %get-tuple-element.45) | copy-start | bytes 6475396
  328.7 3.9 %copy-start.4 = (f32[33,32,511]{2,1,0:T(8,128)S(1)}, f32[33,32,511]{2,1,0:T(8,128)}, u32[]{:S(2)}) copy-start(f32[33,32,511]{2,1,0:T(8,128)} %get-tuple-element.48) | copy-start | bytes 6475396
where the time goes:
time: 360 us; the launch traced here: 353 us
  local copies, waits for them, and re-layouts  185 us (51%)
  other arithmetic  114 us (32%)
  waiting for transfers between devices  31.1 us (9%)
  starting transfers between devices  21.2 us (6%)
    gather x80, local copies, waits for them, and re-layouts  91.2 us
    unnamed x27, local copies, waits for them, and re-layouts  23.9 us
    ppermute x2, waiting for transfers between devices, with_halo(): after = lax.ppermute(leading, axis, down)  22.1 us
    another operation x3, other arithmetic, advance_core(): return jnp.stack([new_x, new_y, new_z], axis=0)  19.4 us
    gather x3, local copies, waits for them, and re-layouts, one_piece(): window = jnp.take(window, pick, axis=3)  18.3 us
    sub x1, other arithmetic, advance_core(): elec_z = velocity[1] * field_x - velocity[0] * field_y  11.3 us
    slice x1, local copies, waits for them, and re-layouts, on_device(): core = extended[:, 1:-1, 1:-1]  11.2 us
    add x3, other arithmetic, prolong(): centre[:, :, None, :, None, :, None]  10.2 us
  transfers between devices with their start and end apart: 5, of which 3 were waited for; matrix products, arithmetic and copies ran while one was open for 21% of the time, Pallas kernels for 0%

commit v1 on v0

v1 whole, which is shorter than its diff:
```python
import functools

import jax
import jax.numpy as jnp
import numpy as np
from jax import lax
from jax.experimental import pallas as pl
from jax.experimental.pallas import tpu as pltpu
from jax.sharding import PartitionSpec as P

F32 = jnp.float32
BF16 = jnp.bfloat16
BS = 16
CAP = 2
PARENTS = 2
KIDS = 16
LANES = 128
LIMIT = 60 * 1024 * 1024

courant = 0.3
SCALE = 0.25 * 0.5 * courant


def even_swap(count):
    return [(i, i ^ 1) for i in range(count)]


def odd_swap(count):
    return [p for i in range(1, count - 1, 2) for p in ((i, i + 1), (i + 1, i))]


def flat_rows(ref):
    rows = 1
    for n in ref.shape[:-1]:
        rows *= n
    return ref.reshape(rows, ref.shape[-1])


def pack_cols_kernel(place, state, even_ref, odd_ref, tiles, sems):
    nx, ny = state.shape[1], state.shape[2]
    nk = state.shape[3] // LANES
    copies = []
    for side in range(2):
        for k in range(nk):
            copies.append(
                pltpu.make_async_copy(
                    state.at[:, :, pl.ds(side * (ny - 8), 8), pl.ds(k * LANES, LANES)],
                    tiles.at[side, k],
                    sems.at[side, k],
                )
            )
    for c in copies:
        c.start()
    for c in copies:
        c.wait()
    high_in_even = place[1] == 0
    for k in range(nk):
        cut = slice(k * LANES, (k + 1) * LANES)
        low_tile = flat_rows(tiles.at[0, k])
        high_tile = flat_rows(tiles.at[1, k])
        for layer in range(9):
            field = layer if layer < 8 else 6
            at_low = field * nx * 8 + (0 if layer < 8 else 1)
            at_high = field * nx * 8 + (7 if layer < 8 else 6)
            low = low_tile[pl.ds(at_low, nx, stride=8), :]
            high = high_tile[pl.ds(at_high, nx, stride=8), :]
            even_ref[layer, :, cut] = jnp.where(high_in_even, high, low)
            odd_ref[layer, :, cut] = jnp.where(high_in_even, low, high)


def pack_cols(place, state):
    fields, nx, ny, nz = state.shape
    shape = jax.ShapeDtypeStruct((fields + 1, nx, nz), F32)
    return pl.pallas_call(
        pack_cols_kernel,
        out_shape=[shape, shape],
        in_specs=[pl.BlockSpec(memory_space=pltpu.SMEM), pl.BlockSpec(memory_space=pl.ANY)],
        out_specs=[pl.BlockSpec(memory_space=pltpu.VMEM)] * 2,
        scratch_shapes=[
            pltpu.VMEM((2, nz // LANES, fields, nx, 8, LANES), F32),
            pltpu.SemaphoreType.DMA((2, nz // LANES)),
        ],
        compiler_params=pltpu.CompilerParams(vmem_limit_bytes=LIMIT),
        name="pack_cols",
    )(place, state)


def pack_rows_kernel(place, state, even_ref, odd_ref, sems):
    nx = state.shape[1]
    at_even = jnp.where(place[0] == 0, nx - 1, 0)
    at_odd = nx - 1 - at_even
    copies = []
    for number, (ref, at) in enumerate(((even_ref, at_even), (odd_ref, at_odd))):
        second = jnp.where(at == 0, 1, nx - 2)
        copies.append(
            pltpu.make_async_copy(state.at[:, at], ref.at[pl.ds(0, 8)], sems.at[number, 0])
        )
        copies.append(pltpu.make_async_copy(state.at[5, second], ref.at[8], sems.at[number, 1]))
    for c in copies:
        c.start()
    for c in copies:
        c.wait()


def pack_rows(place, state):
    fields, nx, ny, nz = state.shape
    shape = jax.ShapeDtypeStruct((fields + 1, ny, nz), F32)
    return pl.pallas_call(
        pack_rows_kernel,
        out_shape=[shape, shape],
        in_specs=[pl.BlockSpec(memory_space=pltpu.SMEM), pl.BlockSpec(memory_space=pl.ANY)],
        out_specs=[pl.BlockSpec(memory_space=pltpu.VMEM)] * 2,
        scratch_shapes=[pltpu.SemaphoreType.DMA((2, 2))],
        compiler_params=pltpu.CompilerParams(vmem_limit_bytes=LIMIT),
        name="pack_rows",
    )(place, state)


def lane_up(parts, lane):
    rolled = [pltpu.roll(p, LANES - 1, 1) for p in parts]
    rolled.append(jnp.zeros_like(parts[0]))
    return [jnp.where(lane == LANES - 1, rolled[k + 1], rolled[k]) for k in range(len(parts))]


def lane_down(parts, lane):
    rolled = [pltpu.roll(p, 1, 1) for p in parts]
    rolled = [jnp.zeros_like(parts[0])] + rolled
    return [jnp.where(lane == 0, rolled[k], rolled[k + 1]) for k in range(len(parts))]


def advance_kernel(
    place, state, row_even, row_odd, col_even, col_odd, cor_even, cor_odd,
    out, dens, flds, rims, rim_e, edge, prev, done, in_sems, halo_sems, out_sems,
):
    nx, ny, nz = state.shape[1:]
    nk = nz // LANES
    chunk = 4
    chunks = nx // chunk
    row_par, col_par = place[0], place[1]

    def cut(k):
        return slice(k * LANES, (k + 1) * LANES)

    def chunk_in(c):
        at = pl.ds(c * chunk, chunk)
        to = pl.ds(1 + c * chunk, chunk)
        return (
            pltpu.make_async_copy(state.at[0, at], dens.at[to], in_sems.at[c, 0]),
            pltpu.make_async_copy(state.at[pl.ds(2, 6), at], flds.at[:, to], in_sems.at[c, 1]),
        )

    def rows_in(source, side):
        to = 0 if side == 0 else nx + 1
        copies = [
            pltpu.make_async_copy(source.at[0], dens.at[to], halo_sems.at[side, 0]),
            pltpu.make_async_copy(source.at[pl.ds(2, 6)], flds.at[:, to], halo_sems.at[side, 1]),
        ]
        if side == 1:
            copies.append(
                pltpu.make_async_copy(source.at[8], flds.at[3, nx + 2], halo_sems.at[side, 2])
            )
        return copies

    def cols_in(source, side):
        return [pltpu.make_async_copy(source, rims.at[side, :, pl.ds(8, nx)], halo_sems.at[side, 3])]

    def corner_in(source, half, side, end):
        to = pl.ds(0 if end == 0 else nx + 8, 8)
        return [
            pltpu.make_async_copy(source.at[half], rims.at[side, :, to], halo_sems.at[side, 4 + end])
        ]

    for side in range(2):
        @pl.when(row_par == side)
        def _():
            for c in rows_in(row_odd, side):
                c.start()

        @pl.when(row_par != side)
        def _():
            for c in rows_in(row_even, side):
                c.start()

        @pl.when(col_par == side)
        def _():
            for c in cols_in(col_odd, side):
                c.start()

        @pl.when(col_par != side)
        def _():
            for c in cols_in(col_even, side):
                c.start()

        half = jnp.where(col_par == side, 1, 0)
        for end in range(2):
            @pl.when(row_par == end)
            def _():
                for c in corner_in(cor_odd, half, side, end):
                    c.start()

            @pl.when(row_par != end)
            def _():
                for c in corner_in(cor_even, half, side, end):
                    c.start()

    for c in range(chunks):
        for copy in chunk_in(c):
            copy.start()

    for side in range(2):
        for c in rows_in(row_even, side) + cols_in(col_even, side):
            c.wait()
        for end in range(2):
            for c in corner_in(cor_even, 0, side, end):
                c.wait()

    lane = lax.broadcasted_iota(jnp.int32, (ny, LANES), 1)
    row = lax.broadcasted_iota(jnp.int32, (ny, LANES), 0)

    for at in (0, nx + 1):
        dens[at] = jnp.where(dens[at] > 0.0, dens[at], 1.0)

    span = rims.shape[2]
    rim_lane = lax.broadcasted_iota(jnp.int32, (span, LANES), 1)
    for side in range(2):
        face_z = [rims[side, 7, :, cut(k)] for k in range(nk)]
        face_z_up = lane_up(face_z, rim_lane)
        for k in range(nk):
            rho = rims[side, 0, :, cut(k)]
            inv = SCALE / jnp.where(rho > 0.0, rho, 1.0)
            vel_x = rims[side, 2, :, cut(k)] * inv
            vel_y = rims[side, 3, :, cut(k)] * inv
            vel_z = rims[side, 4, :, cut(k)] * inv
            face_x = rims[side, 5, :, cut(k)]
            mag_x = face_x + pltpu.roll(face_x, span - 1, 0)
            mag_z = face_z[k] + face_z_up[k]
            mag_y = rims[side, 6, :, cut(k)]
            if side == 1:
                rim_e[3, 0, k] = mag_y
                mag_y = mag_y + rims[side, 8, :, cut(k)]
            rim_e[side, 0, k] = vel_y * mag_x - vel_x * mag_y
            rim_e[side, 1, k] = vel_z * mag_y - vel_y * mag_z
            if side == 0:
                rim_e[2, 0, k] = vel_x
                rim_e[2, 1, k] = vel_z

    prev[...] = jnp.zeros_like(prev)

    def plane(p, carry):
        @pl.when((p % chunk == 0) & (p < nx))
        def _():
            for copy in chunk_in(p // chunk):
                copy.wait()

        at_rim = pl.ds(p + 7, 1)
        face_z = [flds[5, p, :, cut(k)] for k in range(nk)]
        face_z_up = lane_up(face_z, lane)
        elec_y = []
        for k in range(nk):
            inv = SCALE / dens[p, :, cut(k)]
            vel_x = flds[0, p, :, cut(k)] * inv
            vel_y = flds[1, p, :, cut(k)] * inv
            vel_z = flds[2, p, :, cut(k)] * inv
            face_y = flds[4, p, :, cut(k)]
            mag_x = flds[3, p, :, cut(k)] + flds[3, p + 1, :, cut(k)]
            above = jnp.where(
                row == ny - 1, rim_e[3, 0, k, at_rim], pltpu.roll(face_y, ny - 1, 0)
            )
            mag_y = face_y + above
            mag_z = face_z[k] + face_z_up[k]
            edge[0, k, 8 : ny + 8] = vel_y * mag_x - vel_x * mag_y
            edge[1, k, 8 : ny + 8] = vel_z * mag_y - vel_y * mag_z
            elec_y.append(vel_x * mag_z - vel_z * mag_x)
            first = face_y[0:1]
            edge[0, k, 7:8] = rim_e[0, 0, k, at_rim] - rim_e[2, 0, k, at_rim] * first
            edge[1, k, 7:8] = rim_e[0, 1, k, at_rim] + rim_e[2, 1, k, at_rim] * first
            edge[0, k, ny + 8 : ny + 9] = rim_e[1, 0, k, at_rim]
            edge[1, k, ny + 8 : ny + 9] = rim_e[1, 1, k, at_rim]
        y_down = lane_down(elec_y, lane)
        y_up = lane_up(elec_y, lane)
        before = jnp.maximum(p - 1, 0)
        for k in range(nk):
            z_below = edge[0, k, 7 : ny + 7]
            z_here = edge[0, k, 8 : ny + 8]
            z_above = edge[0, k, 9 : ny + 9]
            turn = (z_above - z_below) - (y_up[k] - y_down[k])
            z_sum = z_below + z_here
            y_sum = y_down[k] + elec_y[k]
            done[0, p, :, cut(k)] = flds[3, p, :, cut(k)] - (prev[0, k] + turn)
            done[1, before, :, cut(k)] = done[1, before, :, cut(k)] + z_sum
            done[2, before, :, cut(k)] = done[2, before, :, cut(k)] - y_sum
            done[1, p, :, cut(k)] = flds[4, p, :, cut(k)] - prev[1, k]
            done[2, p, :, cut(k)] = face_z[k] + prev[2, k]
            prev[0, k] = turn
            prev[1, k] = z_sum
            prev[2, k] = y_sum
        x_sum = []
        x_diff = []
        for k in range(nk):
            below = edge[1, k, 7 : ny + 7]
            x_sum.append(below + edge[1, k, 8 : ny + 8])
            x_diff.append(edge[1, k, 9 : ny + 9] - below)
        sum_down = lane_down(x_sum, lane)
        sum_up = lane_up(x_sum, lane)
        diff_down = lane_down(x_diff, lane)
        for k in range(nk):
            done[1, p, :, cut(k)] = done[1, p, :, cut(k)] - (sum_up[k] - sum_down[k])
            done[2, p, :, cut(k)] = done[2, p, :, cut(k)] + (diff_down[k] + x_diff[k])

        @pl.when((p > chunk) & ((p - 1) % chunk == 0))
        def _():
            chunk_out((p - 1) // chunk - 1).start()

        return carry

    def chunk_out(c):
        return pltpu.make_async_copy(
            done.at[:, pl.ds(1 + c * chunk, chunk)],
            out.at[:, pl.ds(c * chunk, chunk)],
            out_sems.at[c],
        )

    lax.fori_loop(0, nx + 2, plane, 0)
    for c in range(chunks):
        chunk_out(c).wait()


def advance(place, state, rows_halo, cols_halo, corners):
    nx, ny, nz = state.shape[1:]
    nk = nz // LANES
    any_space = pl.BlockSpec(memory_space=pl.ANY)
    return pl.pallas_call(
        advance_kernel,
        out_shape=jax.ShapeDtypeStruct((3, nx, ny, nz), F32),
        in_specs=[pl.BlockSpec(memory_space=pltpu.SMEM)] + [any_space] * 7,
        out_specs=any_space,
        scratch_shapes=[
            pltpu.VMEM((nx + 2, ny, nz), F32),
            pltpu.VMEM((6, nx + 3, ny, nz), F32),
            pltpu.VMEM((2, 9, nx + 16, nz), F32),
            pltpu.VMEM((4, 2, nk, nx + 16, LANES), F32),
            pltpu.VMEM((2, nk, ny + 16, LANES), F32),
            pltpu.VMEM((3, nk, ny, LANES), F32),
            pltpu.VMEM((3, nx + 2, ny, nz), F32),
            pltpu.SemaphoreType.DMA((nx // 4, 2)),
            pltpu.SemaphoreType.DMA((2, 6)),
            pltpu.SemaphoreType.DMA((nx // 4,)),
        ],
        compiler_params=pltpu.CompilerParams(vmem_limit_bytes=LIMIT),
        cost_estimate=pl.CostEstimate(
            flops=60 * nx * ny * nz, bytes_accessed=40 * nx * ny * nz, transcendentals=0
        ),
        name="advance",
    )(place, state, *rows_halo, *cols_halo, *corners)


SIDE = BS // 2 + 2
WIDE = BS + 2


def pieces_kernel(
    place, parent, slots, state, row_even, row_odd, col_even, col_odd, out, window, rim, sems
):
    nx, ny, nz = state.shape[1:]
    nk = nz // LANES
    row_par, col_par = place[0], place[1]
    spots = []
    for r in range(PARENTS):
        ix, iy, kz = parent[3 * r], parent[3 * r + 1], parent[3 * r + 2]
        begin = kz * BS - 1
        tile = (begin + LANES) // LANES - 1
        shift = begin - tile * LANES
        y_from = pl.multiple_of(8 * iy, 8)
        y_to = pl.multiple_of(8 - 8 * iy, 8)
        waits = []
        for t in range(2):
            column = jnp.clip(tile + t, 0, nk - 1)
            z_at = pl.ds(pl.multiple_of(column * LANES, LANES), LANES)
            body = pltpu.make_async_copy(
                state.at[:, pl.ds((BS - 1) * ix, BS + 1), pl.ds(y_from, 24), z_at],
                window.at[r, t, :, pl.ds(1 - ix, BS + 1), pl.ds(y_to, 24)],
                sems.at[r, t, 0],
            )
            body.start()

            def row_copy(source):
                return pltpu.make_async_copy(
                    source.at[pl.ds(0, 8), pl.ds(y_from, 24), z_at],
                    window.at[r, t, :, (WIDE - 1) * ix, pl.ds(y_to, 24)],
                    sems.at[r, t, 1],
                )

            def col_copy(source):
                return pltpu.make_async_copy(
                    source.at[pl.ds(0, 8), pl.ds(pl.multiple_of(ix * BS, BS), BS), z_at],
                    rim.at[r, t],
                    sems.at[r, t, 2],
                )

            @pl.when(ix != row_par)
            def _():
                row_copy(row_even).start()

            @pl.when(ix == row_par)
            def _():
                row_copy(row_odd).start()

            @pl.when(iy != col_par)
            def _():
                col_copy(col_even).start()

            @pl.when(iy == col_par)
            def _():
                col_copy(col_odd).start()

            waits += [body, row_copy(row_even), col_copy(col_even)]
        spots.append((iy, kz, shift, waits))

    out[...] = jnp.zeros_like(out)
    lane = lax.broadcasted_iota(jnp.int32, (8, LANES), 1)
    sub = lax.broadcasted_iota(jnp.int32, (8, LANES), 0)
    filler = jnp.where(sub == 0, 1.0, 0.0)
    for r in range(PARENTS):
        iy, kz, shift, waits = spots[r]
        for w in waits:
            w.wait()
        for t in range(2):
            for at in (0, WIDE - 1):
                rho = window[r, t, 0, at]
                window[r, t, 0, at] = jnp.where(rho > 0.0, rho, 1.0)
        turn = LANES - shift
        first = lane < turn
        outside = ((kz == 0) & (lane == 0)) | ((kz == nz // BS - 1) & (lane == WIDE - 1))
        flat = [flat_rows(window.at[r, t]) for t in range(2)]
        flat_rim = [flat_rows(rim.at[r, t]) for t in range(2)]

        def plane(i, carry):
            inside = (i > 0) & (i < WIDE - 1)
            rim_row = jnp.clip(i - 1, 0, BS - 1)
            sums = [jnp.zeros((8, LANES), F32) for _ in range(4)]
            for j in range(WIDE):
                halves = []
                for t in range(2):
                    value = flat[t][pl.ds(i * 32 + j + 7, 8, stride=WIDE * 32), :]
                    if j == 0 or j == WIDE - 1:
                        beside = flat_rim[t][pl.ds(rim_row, 8, stride=BS), :]
                        beside = jnp.where((sub == 0) & (beside == 0.0), 1.0, beside)
                        from_rim = iy == (0 if j == 0 else 1)
                        value = jnp.where(from_rim, beside, value)
                        value = jnp.where(inside, value, 0.0)
                    halves.append(pltpu.roll(value, turn, 1))
                value = jnp.where(first, halves[0], halves[1])
                value = jnp.where(outside, filler, value)
                parts = (
                    jnp.where(lane < SIDE, value, 0.0),
                    jnp.where((lane >= BS // 2) & (lane < WIDE), value, 0.0),
                )
                for b in range(2):
                    row = j - 8 * b
                    if 0 <= row < SIDE:
                        for c in range(2):
                            amount = (row * SIDE - 8 * c) % LANES
                            moved = pltpu.roll(parts[c], amount, 1) if amount else parts[c]
                            sums[2 * b + c] = sums[2 * b + c] + moved
            for b in range(2):
                for c in range(2):
                    for a in range(2):
                        number = 8 * r + 4 * a + 2 * b + c

                        @pl.when((i >= 8 * a) & (i < 8 * a + SIDE))
                        def _():
                            at = pl.multiple_of((i - 8 * a) * 8, 8)
                            out[slots[number], pl.ds(at, 8)] = sums[2 * b + c]

            return carry

        lax.fori_loop(0, WIDE, plane, 0)


def pieces(place, parent, slots, state, rows_halo, cols_halo, count):
    smem = pl.BlockSpec(memory_space=pltpu.SMEM)
    any_space = pl.BlockSpec(memory_space=pl.ANY)
    return pl.pallas_call(
        pieces_kernel,
        out_shape=jax.ShapeDtypeStruct((count * CAP, SIDE * 8, LANES), F32),
        in_specs=[smem] * 3 + [any_space] * 5,
        out_specs=pl.BlockSpec(memory_space=pltpu.VMEM),
        scratch_shapes=[
            pltpu.VMEM((PARENTS, 2, 8, WIDE, 32, LANES), F32),
            pltpu.VMEM((PARENTS, 2, 8, BS, LANES), F32),
            pltpu.SemaphoreType.DMA((PARENTS, 2, 3)),
        ],
        compiler_params=pltpu.CompilerParams(vmem_limit_bytes=LIMIT),
        name="pieces",
    )(place, parent, slots, state, *rows_halo, *cols_halo)


def spread_weights():
    spread = np.zeros((3, LANES, 256), np.float32)
    for y in range(BS):
        for z in range(BS):
            at = (y // 2 + 1) * SIDE + z // 2 + 1
            spread[0, at, y * BS + z] = 1.0
            spread[1, at, y * BS + z] = 0.25 * (2 * (y % 2) - 1)
            spread[2, at, y * BS + z] = 0.25 * (2 * (z % 2) - 1)
    return spread


def limited(left, right):
    return jnp.maximum(jnp.minimum(left, right), 0.0) + jnp.minimum(jnp.maximum(left, right), 0.0)


def thirds(value):
    top = value.astype(BF16)
    rest = value - top.astype(F32)
    middle = rest.astype(BF16)
    return top, middle, (rest - middle.astype(F32)).astype(BF16)


def prolong_kernel(weights, piece, out, low, high, side):
    count = piece.shape[0]
    sub = lax.broadcasted_iota(jnp.int32, (64, LANES), 0) % 8
    cells = sub < 5

    def slopes(s, carry):
        here = piece[s, 8:72]
        x_up = piece[s, 16:80] - here
        x_down = here - piece[s, 0:64]
        y_up = pltpu.roll(here, LANES - SIDE, 1) - here
        y_down = here - pltpu.roll(here, SIDE, 1)
        z_up = pltpu.roll(here, LANES - 1, 1) - here
        z_down = here - pltpu.roll(here, 1, 1)
        slope_x = jnp.where(cells, limited(x_up, x_down), jnp.where(sub == 5, x_up, 0.0))
        slope_y = jnp.where(cells, limited(y_up, y_down), jnp.where(sub == 6, y_up, 0.0))
        slope_z = jnp.where(cells, limited(z_up, z_down), jnp.where(sub == 7, z_up, 0.0))
        middle = here + jnp.where(cells, 0.0, 0.25 * (slope_x + slope_y + slope_z))
        at = pl.ds(pl.multiple_of(s * 64, 64), 64)
        low[at] = middle - 0.25 * slope_x
        high[at] = middle + 0.25 * slope_x
        side[at, 0:LANES] = slope_y
        side[at, LANES:] = slope_z
        return carry

    lax.fori_loop(0, count, slopes, 0)
    spread = weights[0]
    both = weights[1:3].reshape(2 * LANES, 256)

    def times(value, matrix):
        return sum(jnp.dot(v, matrix, preferred_element_type=F32) for v in thirds(value))

    for s in range(count):
        at = slice(s * 64, (s + 1) * 64)
        tilt = times(side[at], both)
        for p, half in enumerate((low, high)):
            fine = times(half[at], spread) + tilt
            for i in range(8):
                x = 2 * i + p
                out[0, 0, s // 2, s % 2, :, x * 256 : (x + 1) * 256] = fine[8 * i : 8 * i + 8]


def prolong(received, count):
    group = 8
    return pl.pallas_call(
        prolong_kernel,
        grid=(count * CAP // group,),
        out_shape=jax.ShapeDtypeStruct((1, 1, count, CAP, 8, BS**3), F32),
        in_specs=[
            pl.BlockSpec((3, LANES, 256), lambda g: (0, 0, 0)),
            pl.BlockSpec((group, SIDE * 8, LANES), lambda g: (g, 0, 0)),
        ],
        out_specs=pl.BlockSpec(
            (1, 1, group // CAP, CAP, 8, BS**3), lambda g: (0, 0, g, 0, 0, 0)
        ),
        scratch_shapes=[
            pltpu.VMEM((group * 64, LANES), F32),
            pltpu.VMEM((group * 64, LANES), F32),
            pltpu.VMEM((group * 64, 2 * LANES), F32),
        ],
        compiler_params=pltpu.CompilerParams(vmem_limit_bytes=LIMIT),
        name="prolong",
    )(jnp.asarray(spread_weights(), BF16), received)


def find_parents(flags):
    gx, gy, gz = flags.shape
    where = jnp.arange(gx * gy * gz, dtype=jnp.int32).reshape(flags.shape)
    first = jnp.min(jnp.where(flags == 1, where, gx * gy * gz - 1))
    last = jnp.max(jnp.where(flags == 1, where, 0))
    at = jnp.stack([first, last])
    return jnp.stack([at // (gy * gz), at // gz % gy, at % gz], axis=1).reshape(-1)


def find_slots(owners):
    same = owners[:, None] == owners[None, :]
    number = jnp.arange(owners.shape[0])
    earlier = same & (number[None, :] < number[:, None])
    return owners * CAP + jnp.sum(earlier.astype(jnp.int32), axis=1)


def on_device(state, flags, owners):
    rows, cols = lax.axis_size("rows"), lax.axis_size("cols")
    place = jnp.stack([lax.axis_index("rows") % 2, lax.axis_index("cols") % 2]).astype(jnp.int32)
    col_even, col_odd = pack_cols(place, state)
    col_even = lax.ppermute(col_even, "cols", even_swap(cols))
    col_odd = lax.ppermute(col_odd, "cols", odd_swap(cols))
    row_even, row_odd = pack_rows(place, state)
    row_even = lax.ppermute(row_even, "rows", even_swap(rows))
    row_odd = lax.ppermute(row_odd, "rows", odd_swap(rows))

    parent = find_parents(flags)
    slots = find_slots(owners[:, 0])
    sent = pieces(
        place, parent, slots, state, (row_even, row_odd), (col_even, col_odd), cols
    )
    received = lax.all_to_all(
        sent.reshape((cols, CAP) + sent.shape[1:]), "cols", split_axis=0, concat_axis=0, tiled=True
    )

    both = jnp.stack([col_even, col_odd])
    low, high = both[:, :, :8], both[:, :, -8:]
    cor_even = lax.ppermute(jnp.where(place[0] == 0, high, low), "rows", even_swap(rows))
    cor_odd = lax.ppermute(jnp.where(place[0] == 0, low, high), "rows", odd_swap(rows))
    faces_new = advance(
        place, state, (row_even, row_odd), (col_even, col_odd), (cor_even, cor_odd)
    )
    arrivals = prolong(received.reshape(sent.shape), cols)
    return faces_new, arrivals


def solution(mesh):
    return jax.shard_map(
        on_device,
        mesh=mesh,
        in_specs=(
            P(None, "rows", "cols", None),
            P("rows", "cols", None),
            P(("rows", "cols"), None),
        ),
        out_specs=(P(None, "rows", "cols", None), P("rows", "cols", None, None, None, None)),
        check_vma=False,
    )
```

time: 360 us -> 89.5 us (0.25)
  the two profiles are of different devices: /device:TPU:8 before, /device:TPU:1 now
where the time goes in v1:
time: 89.5 us; the launch traced here: 89.1 us
  Pallas kernels  48.3 us (54%)
  starting transfers between devices  21.9 us (24%)
  waiting for transfers between devices  8.63 us (10%)
  other arithmetic  6.08 us (7%)
  local copies, waits for them, and re-layouts  3.33 us (4%)
    pallas_call x1, Pallas kernels, advance(): pl.pallas_call(advance_kernel, out_shape=jax.ShapeDtypeStruct((3, nx, ny,...  16.3 us
    pallas_call x1, Pallas kernels, pieces(): pl.pallas_call(pieces_kernel, out_shape=jax.ShapeDtypeStruct((count * CAP...  13.4 us
    pallas_call x1, Pallas kernels, prolong(): pl.pallas_call(prolong_kernel, grid=(count * CAP // group,), out_shape=ja...  10.1 us
    all_to_all x1, starting transfers between devices, on_device(): lax.all_to_all(sent.reshape((cols, CAP) + sent.shape[1:]), 'cols', split_...  10 us
    pallas_call x1, Pallas kernels, pack_cols(): pl.pallas_call(pack_cols_kernel, out_shape=[shape, shape], in_specs=[pl.B...  5.47 us
    ppermute x1, waiting for transfers between devices, on_device(): lax.ppermute(jnp.where(place[0] == 0, low, high), 'rows', odd_swap(rows))  5.19 us
    ppermute x1, waiting for transfers between devices, on_device(): row_odd = lax.ppermute(row_odd, 'rows', odd_swap(rows))  3.42 us
    ppermute x1, starting transfers between devices, on_device(): lax.ppermute(jnp.where(place[0] == 0, low, high), 'rows', odd_swap(rows))  3.1 us
  transfers between devices with their start and end apart: 7, of which 2 were waited for; matrix products, arithmetic and copies ran while one was open for 7% of the time, Pallas kernels for 22%

profile of v1, /device:TPU:1, one launch (start us, length us, event | category | flops | bytes accessed | tf_op | source)
XLA Modules:
  0.0 89.1 jit_solution(11552373287463974102)
XLA Ops:
  0.6 0.7 pad_add_fusion.2.place
  1.3 5.5 %pack_cols.1 = (f32[9,32,512]{2,1,0:T(8,128)}, f32[9,32,512]{2,1,0:T(8,128)}) custom-call(s32[2]{0:T(128)} %pad_add_fusion.2.place, f32[8,32,32,512]{3,2,1,0:T(8,128)} %state.7), custom_call_target="tpu_custom_call" | custom-call | tf_op jit(solution)/shard_map/pack_cols/pallas_call | solution.py:74
  6.8 2.1 %collective-permute-start.2 = (f32[9,32,512]{2,1,0:T(8,128)}, f32[9,32,512]{2,1,0:T(8,128)S(1)}, u32[]{:S(2)}, u32[]{:S(2)}) collective-permute-start(f32[9,32,512]{2,1,0:T(8,128)} %get-tuple-element.8), channel_id=1, source_target_pairs={{0,1},{1,0},{2,3},{3,2},{4,5},{5,4},{6,7},{7,6},{8,9},{9,8},{10,11... | collective-permute-start | bytes 1769480 | tf_op jit(solution)/shard_map/ppermute | solution.py:604
  8.9 0.8 collective-permute-start.3
  9.7 2.9 %pack_rows.1 = (f32[9,32,512]{2,1,0:T(8,128)}, f32[9,32,512]{2,1,0:T(8,128)}) custom-call(s32[2]{0:T(128)} %pad_add_fusion.2.place, f32[8,32,32,512]{3,2,1,0:T(8,128)} %state.7), custom_call_target="tpu_custom_call" | custom-call | tf_op jit(solution)/shard_map/pack_rows/pallas_call | solution.py:108
  12.7 1.0 %collective-permute-start = (f32[9,32,512]{2,1,0:T(8,128)}, f32[9,32,512]{2,1,0:T(8,128)S(1)}, u32[]{:S(2)}, u32[]{:S(2)}) collective-permute-start(f32[9,32,512]{2,1,0:T(8,128)} %get-tuple-element.6), channel_id=1, source_target_pairs={{0,16},{16,0},{32,48},{48,32},{64,80},{80,64},{96,112},{112,96},{1... | collective-permute-start | bytes 1769480 | tf_op jit(solution)/shard_map/ppermute | solution.py:607
  13.7 3.1 %collective-permute-start.1 = (f32[9,32,512]{2,1,0:T(8,128)}, f32[9,32,512]{2,1,0:T(8,128)S(1)}, u32[]{:S(2)}, u32[]{:S(2)}) collective-permute-start(f32[9,32,512]{2,1,0:T(8,128)} %get-tuple-element.7), channel_id=1, source_target_pairs={{16,32},{32,16},{48,64},{64,48},{80,96},{96,80},{17,33},{33,17},{4... | collective-permute-start | bytes 1769480 | tf_op jit(solution)/shard_map/ppermute | solution.py:608
  16.8 0.7 select_reduce_fusion.1
  17.6 1.3 %and_select_fusion.3 = s32[2,1]{1,0:T(2,128)S(1)} fusion(s32[1,1]{1,0:T(1,128)} %bitcast.5, s32[1,1]{1,0:T(1,128)} %bitcast.4), kind=kLoop, calls=%fused_computation.15 | loop fusion | flops 32 | bytes 16 | tf_op jit(solution)/shard_map/jit(floor_divide)/jit(_where)/select_n | solution.py:590
  18.9 1.3 %and_select_fusion = (s32[2,1]{1,0:T(2,128)S(1)}, s32[2,1]{1,0:T(2,128)S(1)}) fusion(s32[1,1]{1,0:T(1,128)} %bitcast.5, s32[1,1]{1,0:T(1,128)} %bitcast.4), kind=kLoop, calls=%fused_computation.12 | loop fusion | flops 62 | bytes 24 | tf_op jit(solution)/shard_map/jit(remainder)/select_n | solution.py:590
  20.2 0.1 pad_add_fusion.1
  20.3 0.7 reshape.372.parent
  21.0 0.2 convert_reduce_fusion
  21.1 0.5 multiply_add_fusion.1.slots
  21.7 0.0 collective-permute-done.2.col_even
  21.7 0.0 collective-permute-done.3.col_odd
  21.7 0.0 collective-permute-done.row_even
  21.7 3.4 %collective-permute-done.1.row_odd = f32[9,32,512]{2,1,0:T(8,128)S(1)} collective-permute-done((f32[9,32,512]{2,1,0:T(8,128)}, f32[9,32,512]{2,1,0:T(8,128)S(1)}, u32[]{:S(2)}, u32[]{:S(2)}) %collective-permute-start.1) | collective-permute-done | bytes 589856 | tf_op jit(solution)/shard_map/ppermute | solution.py:608
  25.1 0.0 copy-done.1
  25.1 0.8 copy-done.4
  26.0 13.4 %pieces.1 = f32[32,80,128]{2,1,0:T(8,128)} custom-call(s32[2]{0:T(128)} %pad_add_fusion.2.place, s32[6]{0:T(128)} %reshape.372.parent, s32[16]{0:T(128)} %multiply_add_fusion.1.slots, f32[8,32,32,512]{3,2,1,0:T(8,128)} %state.7, f32[9,32,512]{2,1,0:T(8,128)} %copy-done.3, f32[9,32,512]{2,1,0:T(8,128)} %copy-done.4, f32[9,32,512]{2,1,0:T(8,128)} %copy-done, ...), custom_call_target="tpu_custom_call" | custom-call | tf_op jit(solution)/shard_map/pieces/pallas_call | solution.py:483
  39.4 10.0 %all-to-all-start = ((f32[16,2,80,128]{3,2,1,0:T(8,128)}), f32[16,2,80,128]{3,2,1,0:T(8,128)S(1)}, u32[]{:S(2)}, u32[]{:S(2)}) async-start(f32[16,2,80,128]{3,2,1,0:T(8,128)} %bitcast.12), calls=%async_computation | async-start | bytes 2621440 | tf_op jit(solution)/shard_map/all_to_all | solution.py:615
  49.4 1.2 %broadcast_select_fusion = (f32[2,9,8,512]{3,2,1,0:T(8,128)S(1)}, f32[2,9,8,512]{3,2,1,0:T(8,128)S(1)}, f32[2,9,8,512]{3,2,1,0:T(8,128)S(1)}) fusion(pred[]{:T(512)S(6)} %eq.27, f32[1,9,32,512]{3,2,1,0:T(8,128)} %bitcast.11, f32[1,9,32,512]{3,2,1,0:T(8,128)} %bitcast.10), kind=kLoop, calls=%fused_computation.2 | loop fusion | flops 221184 | bytes 2064385 | tf_op jit(solution)/shard_map/jit(_where)/select_n | solution.py:622
  50.7 1.8 %collective-permute-start.4 = (f32[2,9,8,512]{3,2,1,0:T(8,128)S(1)}, f32[2,9,8,512]{3,2,1,0:T(8,128)S(1)}, u32[]{:S(2)}, u32[]{:S(2)}) collective-permute-start(f32[2,9,8,512]{3,2,1,0:T(8,128)S(1)} %broadcast_select_fusion.1), channel_id=1, source_target_pairs={{0,16},{16,0},{32,48},{48,32},{64,80},{80,64},{96,112},{112,96},{1... | collective-permute-start | bytes 884744 | tf_op jit(solution)/shard_map/ppermute | solution.py:621
  52.4 3.1 %collective-permute-start.5 = (f32[2,9,8,512]{3,2,1,0:T(8,128)S(1)}, f32[2,9,8,512]{3,2,1,0:T(8,128)S(1)}, u32[]{:S(2)}, u32[]{:S(2)}) collective-permute-start(f32[2,9,8,512]{3,2,1,0:T(8,128)S(1)} %get-tuple-element.12), channel_id=1, source_target_pairs={{16,32},{32,16},{48,64},{64,48},{80,96},{96,80},{17,33},{33,17},{4... | collective-permute-start | bytes 884744 | tf_op jit(solution)/shard_map/ppermute | solution.py:622
  55.5 0.0 collective-permute-done.4.cor_even
  55.6 5.2 %collective-permute-done.5.cor_odd = f32[2,9,8,512]{3,2,1,0:T(8,128)S(1)} collective-permute-done((f32[2,9,8,512]{3,2,1,0:T(8,128)S(1)}, f32[2,9,8,512]{3,2,1,0:T(8,128)S(1)}, u32[]{:S(2)}, u32[]{:S(2)}) %collective-permute-start.5) | collective-permute-done | bytes 294944 | tf_op jit(solution)/shard_map/ppermute | solution.py:622
  60.8 0.7 copy-done.6
  61.5 16.3 %advance.1 = f32[3,32,32,512]{3,2,1,0:T(8,128)} custom-call(s32[2]{0:T(128)} %pad_add_fusion.2.place, f32[8,32,32,512]{3,2,1,0:T(8,128)} %state.7, f32[9,32,512]{2,1,0:T(8,128)} %copy-done.3, f32[9,32,512]{2,1,0:T(8,128)} %copy-done.4, f32[9,32,512]{2,1,0:T(8,128)} %copy-done, f32[9,32,512]{2,1,0:T(8,128)} %copy-done.1, f32[2,9,8,512]{3,2,1,0:T(8,128)} %copy-done.5, ...), custom_call_target="tpu_custom_call" | custom-call | flops 31457280 | bytes 20971520 | tf_op jit(solution)/shard_map/advance/pallas_call | solution.py:332
  77.8 0.0 all-to-all-done
  77.9 1.1 %copy-done.2 = f32[16,2,80,128]{3,2,1,0:T(8,128)} copy-done((f32[16,2,80,128]{3,2,1,0:T(8,128)}, f32[16,2,80,128]{3,2,1,0:T(8,128)S(1)}, u32[]{:S(2)}) %copy-start.2) | copy-done | bytes 1310744
  78.9 10.1 %prolong.1 = f32[1,1,16,2,8,4096]{5,4,3,2,1,0:T(8,128)} custom-call(bf16[3,128,256]{2,1,0:T(8,128)(2,1)} %constant.82.clone.weights, f32[32,80,128]{2,1,0:T(8,128)} %bitcast.13), custom_call_target="tpu_custom_call" | custom-call | tf_op jit(solution)/shard_map/prolong/pallas_call | solution.py:563
  (15 shorter events, 0.1 us)
Async XLA Ops:
  6.8 14.9 %collective-permute-start.2 = (f32[9,32,512]{2,1,0:T(8,128)}, f32[9,32,512]{2,1,0:T(8,128)S(1)}, u32[]{:S(2)}, u32[]{:S(2)}) collective-permute-start(f32[9,32,512]{2,1,0:T(8,128)} %get-tuple-element.8), channel_id=1, source_target_pairs={{0,1},{1,0},{2,3},{3,2},{4,5},{5,4},{6,7},{7,6},{8,9},{9,8},{10,11... | collective-permute-start | bytes 1769480 | tf_op jit(solution)/shard_map/ppermute | solution.py:604
  8.9 7.9 %copy-start.7 = (s32[2,2,32]{2,1,0:T(2,128)S(1)}, s32[2,2,32]{2,1,0:T(2,128)}, u32[]{:S(2)}) copy-start(s32[2,2,32]{2,1,0:T(2,128)} %param.5) | copy-start | bytes 1540
  8.9 12.0 %copy-start.8 = (s32[16,1]{0,1:T(1,128)S(1)}, s32[16,1]{0,1:T(1,128)}, u32[]{:S(2)}) copy-start(s32[16,1]{0,1:T(1,128)} %param.6) | copy-start | bytes 196
  8.9 12.8 %collective-permute-start.3 = (f32[9,32,512]{2,1,0:T(8,128)}, f32[9,32,512]{2,1,0:T(8,128)S(1)}, u32[]{:S(2)}, u32[]{:S(2)}) collective-permute-start(f32[9,32,512]{2,1,0:T(8,128)} %get-tuple-element.9), channel_id=1, source_target_pairs={{1,2},{2,1},{3,4},{4,3},{5,6},{6,5},{7,8},{8,7},{9,10},{10,9},{11,... | collective-permute-start | bytes 1769480 | tf_op jit(solution)/shard_map/ppermute | solution.py:605
  12.7 9.0 %collective-permute-start = (f32[9,32,512]{2,1,0:T(8,128)}, f32[9,32,512]{2,1,0:T(8,128)S(1)}, u32[]{:S(2)}, u32[]{:S(2)}) collective-permute-start(f32[9,32,512]{2,1,0:T(8,128)} %get-tuple-element.6), channel_id=1, source_target_pairs={{0,16},{16,0},{32,48},{48,32},{64,80},{80,64},{96,112},{112,96},{1... | collective-permute-start | bytes 1769480 | tf_op jit(solution)/shard_map/ppermute | solution.py:607
  13.7 11.4 %collective-permute-start.1 = (f32[9,32,512]{2,1,0:T(8,128)}, f32[9,32,512]{2,1,0:T(8,128)S(1)}, u32[]{:S(2)}, u32[]{:S(2)}) collective-permute-start(f32[9,32,512]{2,1,0:T(8,128)} %get-tuple-element.7), channel_id=1, source_target_pairs={{16,32},{32,16},{48,64},{64,48},{80,96},{96,80},{17,33},{33,17},{4... | collective-permute-start | bytes 1769480 | tf_op jit(solution)/shard_map/ppermute | solution.py:608
  21.7 3.5 %copy-start = (f32[9,32,512]{2,1,0:T(8,128)}, f32[9,32,512]{2,1,0:T(8,128)S(1)}, u32[]{:S(2)}) copy-start(f32[9,32,512]{2,1,0:T(8,128)S(1)} %collective-permute-done.2.col_even) | copy-start | bytes 1769476
  21.7 3.5 %copy-start.1 = (f32[9,32,512]{2,1,0:T(8,128)}, f32[9,32,512]{2,1,0:T(8,128)S(1)}, u32[]{:S(2)}) copy-start(f32[9,32,512]{2,1,0:T(8,128)S(1)} %collective-permute-done.3.col_odd) | copy-start | bytes 1769476
  21.7 3.4 %copy-start.3 = (f32[9,32,512]{2,1,0:T(8,128)}, f32[9,32,512]{2,1,0:T(8,128)S(1)}, u32[]{:S(2)}) copy-start(f32[9,32,512]{2,1,0:T(8,128)S(1)} %collective-permute-done.row_even) | copy-start | bytes 1769476
  25.1 0.8 copy-start.4
  39.4 38.5 %all-to-all-start = ((f32[16,2,80,128]{3,2,1,0:T(8,128)}), f32[16,2,80,128]{3,2,1,0:T(8,128)S(1)}, u32[]{:S(2)}, u32[]{:S(2)}) async-start(f32[16,2,80,128]{3,2,1,0:T(8,128)} %bitcast.12), calls=%async_computation | async-start | bytes 2621440 | tf_op jit(solution)/shard_map/all_to_all | solution.py:615
  50.7 4.9 %collective-permute-start.4 = (f32[2,9,8,512]{3,2,1,0:T(8,128)S(1)}, f32[2,9,8,512]{3,2,1,0:T(8,128)S(1)}, u32[]{:S(2)}, u32[]{:S(2)}) collective-permute-start(f32[2,9,8,512]{3,2,1,0:T(8,128)S(1)} %broadcast_select_fusion.1), channel_id=1, source_target_pairs={{0,16},{16,0},{32,48},{48,32},{64,80},{80,64},{96,112},{112,96},{1... | collective-permute-start | bytes 884744 | tf_op jit(solution)/shard_map/ppermute | solution.py:621
  52.4 8.3 %collective-permute-start.5 = (f32[2,9,8,512]{3,2,1,0:T(8,128)S(1)}, f32[2,9,8,512]{3,2,1,0:T(8,128)S(1)}, u32[]{:S(2)}, u32[]{:S(2)}) collective-permute-start(f32[2,9,8,512]{3,2,1,0:T(8,128)S(1)} %get-tuple-element.12), channel_id=1, source_target_pairs={{16,32},{32,16},{48,64},{64,48},{80,96},{96,80},{17,33},{33,17},{4... | collective-permute-start | bytes 884744 | tf_op jit(solution)/shard_map/ppermute | solution.py:622
  55.5 5.2 %copy-start.5 = (f32[2,9,8,512]{3,2,1,0:T(8,128)}, f32[2,9,8,512]{3,2,1,0:T(8,128)S(1)}, u32[]{:S(2)}) copy-start(f32[2,9,8,512]{3,2,1,0:T(8,128)S(1)} %collective-permute-done.4.cor_even) | copy-start | bytes 884740
  60.7 0.7 copy-start.6
  77.8 1.1 %copy-start.2 = (f32[16,2,80,128]{3,2,1,0:T(8,128)}, f32[16,2,80,128]{3,2,1,0:T(8,128)S(1)}, u32[]{:S(2)}) copy-start(f32[16,2,80,128]{3,2,1,0:T(8,128)S(1)} %all-to-all-done) | copy-start | bytes 3932164

commit v2 on v1

v2 whole, which is shorter than its diff:
```python
import functools

import jax
import jax.numpy as jnp
import numpy as np
from jax import lax
from jax.experimental import pallas as pl
from jax.experimental.pallas import tpu as pltpu
from jax.sharding import PartitionSpec as P

F32 = jnp.float32
BF16 = jnp.bfloat16
BS = 16
CAP = 2
PARENTS = 2
KIDS = 16
LANES = 128
MIB = 1024 * 1024
ANY = pl.BlockSpec(memory_space=pl.ANY)
SMEM = pl.BlockSpec(memory_space=pltpu.SMEM)

courant = 0.3
SCALE = 0.25 * 0.5 * courant


def even_swap(count):
    return [(i, i ^ 1) for i in range(count)]


def odd_swap(count):
    return [p for i in range(1, count - 1, 2) for p in ((i, i + 1), (i + 1, i))]


def flat_rows(ref):
    rows = 1
    for n in ref.shape[:-1]:
        rows *= n
    return ref.reshape(rows, ref.shape[-1])


def parity(axis):
    return lax.rem(lax.axis_index(axis), 2)


def pack_kernel(state, row_even, row_odd, col_even, col_odd, tiles, rims, row_sems, sems, out_sems):
    nx, ny = state.shape[1], state.shape[2]
    nk = state.shape[3] // LANES

    def tile_in(side, k, f):
        return pltpu.make_async_copy(
            state.at[pl.ds(f, 2), :, pl.ds(side * (ny - 8), 8), pl.ds(k * LANES, LANES)],
            tiles.at[side, k, pl.ds(f, 2)],
            sems.at[side, k, f],
        )

    for k in range(nk):
        for side in range(2):
            for f in range(0, 8, 2):
                tile_in(side, k, f).start()
    at_even = jnp.where(parity("rows") == 0, nx - 1, 0)
    at_odd = nx - 1 - at_even
    row_copies = []
    for number, (ref, at) in enumerate(((row_even, at_even), (row_odd, at_odd))):
        second = jnp.where(at == 0, 1, nx - 2)
        row_copies.append(
            pltpu.make_async_copy(state.at[:, at], ref.at[pl.ds(0, 8)], row_sems.at[number, 0])
        )
        row_copies.append(
            pltpu.make_async_copy(state.at[5, second], ref.at[8], row_sems.at[number, 1])
        )
    for c in row_copies:
        c.start()
    high_in_even = parity("cols") == 0
    outs = []
    for k in range(nk):
        for side in range(2):
            for f in range(0, 8, 2):
                tile_in(side, k, f).wait()
        low_tile = flat_rows(tiles.at[0, k])
        high_tile = flat_rows(tiles.at[1, k])
        for layer in range(9):
            field = layer if layer < 8 else 6
            at_low = field * nx * 8 + (0 if layer < 8 else 1)
            at_high = field * nx * 8 + (7 if layer < 8 else 6)
            low = low_tile[pl.ds(at_low, nx, stride=8), :]
            high = high_tile[pl.ds(at_high, nx, stride=8), :]
            rims[0, k, layer] = jnp.where(high_in_even, high, low)
            rims[1, k, layer] = jnp.where(high_in_even, low, high)
        for number, ref in enumerate((col_even, col_odd)):
            c = pltpu.make_async_copy(
                rims.at[number, k],
                ref.at[:, :, pl.ds(k * LANES, LANES)],
                out_sems.at[number, k],
            )
            c.start()
            outs.append(c)
    for c in row_copies + outs:
        c.wait()


def pack(state):
    fields, nx, ny, nz = state.shape
    nk = nz // LANES
    row_shape = jax.ShapeDtypeStruct((fields + 1, ny, nz), F32)
    col_shape = jax.ShapeDtypeStruct((fields + 1, nx, nz), F32)
    return pl.pallas_call(
        pack_kernel,
        out_shape=[row_shape, row_shape, col_shape, col_shape],
        in_specs=[ANY],
        out_specs=[pl.BlockSpec(memory_space=pltpu.VMEM)] * 2 + [ANY] * 2,
        scratch_shapes=[
            pltpu.VMEM((2, nk, fields, nx, 8, LANES), F32),
            pltpu.VMEM((2, nk, fields + 1, nx, LANES), F32),
            pltpu.SemaphoreType.DMA((2, 2)),
            pltpu.SemaphoreType.DMA((2, nk, fields)),
            pltpu.SemaphoreType.DMA((2, nk)),
        ],
        compiler_params=pltpu.CompilerParams(vmem_limit_bytes=50 * MIB),
        name="pack",
    )(state)


def lane_up(parts, lane):
    rolled = [pltpu.roll(p, LANES - 1, 1) for p in parts]
    rolled.append(jnp.zeros_like(parts[0]))
    return [jnp.where(lane == LANES - 1, rolled[k + 1], rolled[k]) for k in range(len(parts))]


def lane_down(parts, lane):
    rolled = [pltpu.roll(p, 1, 1) for p in parts]
    rolled = [jnp.zeros_like(parts[0])] + rolled
    return [jnp.where(lane == 0, rolled[k], rolled[k + 1]) for k in range(len(parts))]


def scaled_inverse(rho):
    guess = pl.reciprocal(rho, approx=True)
    guess = guess * (2.0 - rho * guess)
    guess = guess * (2.0 - rho * guess)
    return SCALE * guess


def advance_kernel(
    state, row_even, row_odd, col_even, col_odd, cor_even, cor_odd,
    out, dens, flds, rims, rim_e, edge, prev, done, in_sems, halo_sems, out_sems,
):
    nx, ny, nz = state.shape[1:]
    nk = nz // LANES
    chunk = 4
    chunks = nx // chunk
    ahead = 3
    row_par, col_par = parity("rows"), parity("cols")

    def cut(k):
        return slice(k * LANES, (k + 1) * LANES)

    def chunk_in(c):
        at = pl.ds(c * chunk, chunk)
        to = pl.ds(1 + c * chunk, chunk)
        copies = [pltpu.make_async_copy(state.at[0, at], dens.at[to], in_sems.at[c, 0])]
        for f in range(6):
            copies.append(
                pltpu.make_async_copy(state.at[f + 2, at], flds.at[f, to], in_sems.at[c, f + 1])
            )
        return copies

    def rows_in(source, side):
        to = 0 if side == 0 else nx + 1
        copies = [
            pltpu.make_async_copy(source.at[0], dens.at[to], halo_sems.at[side, 0]),
            pltpu.make_async_copy(source.at[pl.ds(2, 6)], flds.at[:, to], halo_sems.at[side, 1]),
        ]
        if side == 1:
            copies.append(
                pltpu.make_async_copy(source.at[8], flds.at[3, nx + 2], halo_sems.at[side, 2])
            )
        return copies

    def cols_in(source, side):
        return [pltpu.make_async_copy(source, rims.at[side, :, pl.ds(8, nx)], halo_sems.at[side, 3])]

    def corner_in(source, half, side, end):
        to = pl.ds(0 if end == 0 else nx + 8, 8)
        return [
            pltpu.make_async_copy(source.at[half], rims.at[side, :, to], halo_sems.at[side, 4 + end])
        ]

    for side in range(2):
        @pl.when(row_par == side)
        def _():
            for c in rows_in(row_odd, side):
                c.start()

        @pl.when(row_par != side)
        def _():
            for c in rows_in(row_even, side):
                c.start()

        @pl.when(col_par == side)
        def _():
            for c in cols_in(col_odd, side):
                c.start()

        @pl.when(col_par != side)
        def _():
            for c in cols_in(col_even, side):
                c.start()

        half = jnp.where(col_par == side, 1, 0)
        for end in range(2):
            @pl.when(row_par == end)
            def _():
                for c in corner_in(cor_odd, half, side, end):
                    c.start()

            @pl.when(row_par != end)
            def _():
                for c in corner_in(cor_even, half, side, end):
                    c.start()

    for c in range(ahead):
        for copy in chunk_in(c):
            copy.start()

    for side in range(2):
        for c in rows_in(row_even, side) + cols_in(col_even, side):
            c.wait()
        for end in range(2):
            for c in corner_in(cor_even, 0, side, end):
                c.wait()

    for at in (0, nx + 1):
        dens[at] = jnp.where(dens[at] > 0.0, dens[at], 1.0)

    span = rims.shape[2]
    rim_lane = lax.broadcasted_iota(jnp.int32, (span, LANES), 1)
    for side in range(2):
        face_z = [rims[side, 7, :, cut(k)] for k in range(nk)]
        face_z_up = lane_up(face_z, rim_lane)
        for k in range(nk):
            rho = rims[side, 0, :, cut(k)]
            inv = scaled_inverse(jnp.where(rho > 0.0, rho, 1.0))
            vel_x = rims[side, 2, :, cut(k)] * inv
            vel_y = rims[side, 3, :, cut(k)] * inv
            vel_z = rims[side, 4, :, cut(k)] * inv
            face_x = rims[side, 5, :, cut(k)]
            mag_x = face_x + pltpu.roll(face_x, span - 1, 0)
            mag_z = face_z[k] + face_z_up[k]
            mag_y = rims[side, 6, :, cut(k)]
            if side == 1:
                rim_e[3, 0, k] = mag_y
                mag_y = mag_y + rims[side, 8, :, cut(k)]
            rim_e[side, 0, k] = vel_y * mag_x - vel_x * mag_y
            rim_e[side, 1, k] = vel_z * mag_y - vel_y * mag_z
            if side == 0:
                rim_e[2, 0, k] = vel_x
                rim_e[2, 1, k] = vel_z

    prev[...] = jnp.zeros_like(prev)
    lane = lax.broadcasted_iota(jnp.int32, (8, LANES), 1)
    row = lax.broadcasted_iota(jnp.int32, (8, LANES), 0)
    zero = jnp.zeros((8, LANES), F32)
    nj = ny // 8

    def up_of(value):
        rolled = functools.cache(
            lambda k: pltpu.roll(value(k), LANES - 1, 1) if k < nk else zero
        )
        return lambda k: jnp.where(lane == LANES - 1, rolled(k + 1), rolled(k))

    def down_of(value):
        rolled = functools.cache(lambda k: pltpu.roll(value(k), 1, 1) if k >= 0 else zero)
        return lambda k: jnp.where(lane == 0, rolled(k - 1), rolled(k))

    def plane(p, carry):
        @pl.when((p % chunk == 0) & (p < nx))
        def _():
            for copy in chunk_in(p // chunk):
                copy.wait()

        @pl.when((p % chunk == 0) & (p < nx - ahead * chunk))
        def _():
            for copy in chunk_in(p // chunk + ahead):
                copy.start()

        at_rim = pl.ds(p + 7, 1)
        for k in range(nk):
            first = flds[4, p, 0:1, cut(k)]
            edge[0, k, 7:8] = rim_e[0, 0, k, at_rim] - rim_e[2, 0, k, at_rim] * first
            edge[1, k, 7:8] = rim_e[0, 1, k, at_rim] + rim_e[2, 1, k, at_rim] * first
            edge[0, k, ny + 8 : ny + 9] = rim_e[1, 0, k, at_rim]
            edge[1, k, ny + 8 : ny + 9] = rim_e[1, 1, k, at_rim]
        for j in range(nj):
            at = slice(8 * j, 8 * j + 8)
            to = slice(8 * j + 8, 8 * j + 16)
            face_z = functools.cache(lambda k: flds[5, p, at, cut(k)])
            face_z_up = up_of(face_z)
            for k in range(nk):
                inv = scaled_inverse(dens[p, at, cut(k)])
                vel_x = flds[0, p, at, cut(k)] * inv
                vel_y = flds[1, p, at, cut(k)] * inv
                vel_z = flds[2, p, at, cut(k)] * inv
                face_y = flds[4, p, at, cut(k)]
                mag_x = flds[3, p, at, cut(k)] + flds[3, p + 1, at, cut(k)]
                if j < nj - 1:
                    after = flds[4, p, 8 * j + 8 : 8 * j + 9, cut(k)]
                else:
                    after = rim_e[3, 0, k, at_rim]
                mag_y = face_y + jnp.where(row == 7, after, pltpu.roll(face_y, 7, 0))
                mag_z = face_z(k) + face_z_up(k)
                edge[0, k, to] = vel_y * mag_x - vel_x * mag_y
                edge[1, k, to] = vel_z * mag_y - vel_y * mag_z
                edge[2, k, to] = vel_x * mag_z - vel_z * mag_x
        before = jnp.maximum(p - 1, 0)
        for j in range(nj):
            at = slice(8 * j, 8 * j + 8)
            low, mid, high = (slice(8 * j + n, 8 * j + n + 8) for n in (7, 8, 9))
            elec_y = functools.cache(lambda k: edge[2, k, mid])
            x_sum = functools.cache(lambda k: edge[1, k, low] + edge[1, k, mid])
            x_diff = functools.cache(lambda k: edge[1, k, high] - edge[1, k, low])
            y_down, y_up = down_of(elec_y), up_of(elec_y)
            sum_down, sum_up = down_of(x_sum), up_of(x_sum)
            diff_down = down_of(x_diff)
            for k in range(nk):
                z_low = edge[0, k, low]
                below = y_down(k)
                turn = (edge[0, k, high] - z_low) - (y_up(k) - below)
                z_sum = z_low + edge[0, k, mid]
                y_sum = below + elec_y(k)
                done[0, p, at, cut(k)] = flds[3, p, at, cut(k)] - (prev[0, k, at] + turn)
                done[1, before, at, cut(k)] = prev[3, k, at] + z_sum
                done[2, before, at, cut(k)] = prev[4, k, at] - y_sum
                prev[3, k, at] = (flds[4, p, at, cut(k)] - prev[1, k, at]) - (
                    sum_up(k) - sum_down(k)
                )
                prev[4, k, at] = (flds[5, p, at, cut(k)] + prev[2, k, at]) + (
                    diff_down(k) + x_diff(k)
                )
                prev[0, k, at] = turn
                prev[1, k, at] = z_sum
                prev[2, k, at] = y_sum

        @pl.when((p > chunk) & ((p - 1) % chunk == 0))
        def _():
            chunk_out((p - 1) // chunk - 1).start()

        return carry

    def chunk_out(c):
        return pltpu.make_async_copy(
            done.at[:, pl.ds(1 + c * chunk, chunk)],
            out.at[:, pl.ds(c * chunk, chunk)],
            out_sems.at[c],
        )

    lax.fori_loop(0, nx + 2, plane, 0)
    for c in range(chunks):
        chunk_out(c).wait()


def advance(state, rows_halo, cols_halo, corners):
    nx, ny, nz = state.shape[1:]
    nk = nz // LANES
    return pl.pallas_call(
        advance_kernel,
        out_shape=jax.ShapeDtypeStruct((3, nx, ny, nz), F32),
        in_specs=[ANY] * 7,
        out_specs=ANY,
        scratch_shapes=[
            pltpu.VMEM((nx + 2, ny, nz), F32),
            pltpu.VMEM((6, nx + 3, ny, nz), F32),
            pltpu.VMEM((2, 9, nx + 16, nz), F32),
            pltpu.VMEM((4, 2, nk, nx + 16, LANES), F32),
            pltpu.VMEM((3, nk, ny + 16, LANES), F32),
            pltpu.VMEM((5, nk, ny, LANES), F32),
            pltpu.VMEM((3, nx + 2, ny, nz), F32),
            pltpu.SemaphoreType.DMA((nx // 4, 7)),
            pltpu.SemaphoreType.DMA((2, 6)),
            pltpu.SemaphoreType.DMA((nx // 4,)),
        ],
        compiler_params=pltpu.CompilerParams(vmem_limit_bytes=50 * MIB),
        cost_estimate=pl.CostEstimate(
            flops=60 * nx * ny * nz, bytes_accessed=40 * nx * ny * nz, transcendentals=0
        ),
        name="advance",
    )(state, *rows_halo, *cols_halo, *corners)


SIDE = BS // 2 + 2
WIDE = BS + 2


PITCH = (WIDE + 1) * 24


def z_place(kz, nk):
    begin = kz * BS - 1
    tile = (begin + LANES) // LANES - 1
    columns = [
        pl.ds(pl.multiple_of(jnp.clip(tile + t, 0, nk - 1) * LANES, LANES), LANES)
        for t in range(2)
    ]
    return columns, begin - tile * LANES


ROWS = 56
X_ROWS, Y_ROWS, Z_ROWS = slice(32, 40), slice(40, 48), slice(48, 56)


def turned(value, amount):
    return pltpu.roll(value, amount % LANES, 1) if amount % LANES else value


def to_lane(value, amount):
    return pltpu.roll(value, lax.rem(amount + 2 * LANES, LANES), 1)


def lanes_from(lane, first, count):
    first = first % LANES
    return (lane >= first) & (lane < first + count)


def put_z(lane, side, low, high, half, quarter, c):
    at = lane % 8
    here = (lane >= 64) if half else (lane < 64)
    low = turned(low, 64 * half + 2 * quarter + 1 - 8 * c)
    high = turned(high, 64 * half + 2 * quarter - 7 - 8 * c)
    side = jnp.where(here & (at == 2 * quarter), low, side)
    return jnp.where(here & (at == 2 * quarter + 1), high, side)


def own_kernel(state, flags, owners, out, info, window, aligned, sems):
    nx, ny, nz = state.shape[1:]
    nk = nz // LANES
    gx, gy, gz = flags.shape
    grid = (gy, gz)
    number = lax.broadcasted_iota(jnp.int32, grid, 0) * gz + lax.broadcasted_iota(
        jnp.int32, grid, 1
    )
    first = jnp.full(grid, gx * gy * gz - 1, jnp.int32)
    last = jnp.zeros(grid, jnp.int32)
    for x in range(gx):
        flagged = flags[x] == 1
        here = number + x * gy * gz
        first = jnp.minimum(first, jnp.where(flagged, here, gx * gy * gz - 1))
        last = jnp.maximum(last, jnp.where(flagged, here, 0))
    found = (
        jnp.min(first.astype(F32)).astype(jnp.int32),
        jnp.max(last.astype(F32)).astype(jnp.int32),
    )
    spots = []
    for r in range(PARENTS):
        ix, iy, kz = found[r] // (gy * gz), found[r] // gz % gy, found[r] % gz
        columns, shift = z_place(kz, nk)
        y_from = pl.multiple_of(8 * iy, 8)
        copies = []
        for f in range(8):
            for t in range(2):
                copies.append(
                    pltpu.make_async_copy(
                        state.at[f, pl.ds((BS - 1) * ix, BS + 1), pl.ds(y_from, 24), columns[t]],
                        window.at[r, t, f],
                        sems.at[r, t, f],
                    )
                )
        if r == 0:
            for c in copies:
                c.start()
        spots.append((ix, iy, kz, shift, copies))
        info[3 * r], info[3 * r + 1], info[3 * r + 2] = ix, iy, kz

    names = [owners[n, 0] for n in range(KIDS)]
    for n in range(KIDS):
        rank = jnp.int32(0)
        for m in range(n):
            rank = rank + jnp.where(names[m] == names[n], 1, 0)
        info[3 * PARENTS + n] = names[n] * CAP + rank

    lane = lax.broadcasted_iota(jnp.int32, (8, LANES), 1)
    zero = jnp.zeros((8, LANES), F32)
    for r in range(PARENTS):
        ix, iy, kz, shift, copies = spots[r]
        for c in copies:
            c.wait()
        if r + 1 < PARENTS:
            for c in spots[r + 1][4]:
                c.start()
        from_first = lane >= shift
        outside = ((kz == 0) & (lane == shift)) | (
            (kz == nz // BS - 1) & (lane == lax.rem(shift + WIDE - 1, LANES))
        )

        def align(i, carry):
            for f in range(8):
                for y in range(3):
                    rows = slice(8 * y, 8 * y + 8)
                    value = jnp.where(
                        from_first, window[r, 0, f, i, rows], window[r, 1, f, i, rows]
                    )
                    value = jnp.where(outside, 1.0 if f == 0 else 0.0, value)
                    at = pl.multiple_of(f * PITCH + i * 24 + 8 * y, 8)
                    aligned[pl.ds(at, 8)] = value
            return carry

        lax.fori_loop(0, BS + 1, align, 0, unroll=True)

        def pair(number, carry):
            low_x, low_y = number // 2, number % 2
            plane_at = 8 * low_x - 1 + ix
            row_at = 8 * low_y - 1 + 8 * iy
            sums = None
            y_side = [zero, zero]
            z_side = [zero, zero]
            x_side = [zero, zero]
            held = None
            for i in range(SIDE):
                plane = jnp.clip(plane_at + i, 0, BS)
                sums = [zero, zero]
                z_low = [zero, zero]
                z_high = [zero, zero]
                inner = 0 < i < SIDE - 1
                for j in range(SIDE):
                    if not inner and not 0 < j < SIDE - 1:
                        continue
                    base = plane * 24 + jnp.clip(row_at + j, 0, 23)
                    value = aligned[pl.ds(base, 8, stride=PITCH), :]
                    if 0 < j < SIDE - 1:
                        moved = to_lane(value, 8 * (j - 1) - 1 - shift)
                        for c in range(2):
                            first = 8 * (j - 1) + 8 * c
                            sums[c] = jnp.where(lanes_from(lane, first, 8), moved, sums[c])
                            if inner:
                                z_low[c] = jnp.where(
                                    lanes_from(lane, first - 1, 1), moved, z_low[c]
                                )
                                z_high[c] = jnp.where(
                                    lanes_from(lane, first + 8, 1), moved, z_high[c]
                                )
                    else:
                        half, quarter = (i - 1) % 2, (i - 1) // 2
                        first = 64 * half + 16 * quarter + (8 if j else 0)
                        moved = to_lane(value, first - 1 - shift)
                        for c in range(2):
                            y_side[c] = jnp.where(
                                lanes_from(lane, first + 8 * c, 8), moved, y_side[c]
                            )
                for c in range(2):
                    child = 8 * r + 2 * number + c
                    if inner:
                        half, quarter = (i - 1) % 2, (i - 1) // 2
                        z_side[c] = put_z(lane, z_side[c], z_low[c], z_high[c], half, quarter, c)
                        if half:
                            out[child, 8 * quarter : 8 * quarter + 8] = jnp.where(
                                lane < 64, turned(held[c], -8 * c), turned(sums[c], 64 - 8 * c)
                            )
                    elif i:
                        x_side[c] = jnp.where(lane < 64, turned(sums[c], -8 * c), x_side[c])
                    else:
                        x_side[c] = turned(sums[c], 64 - 8 * c)
                held = sums
            for c in range(2):
                child = 8 * r + 2 * number + c
                out[child, X_ROWS] = x_side[c]
                out[child, Y_ROWS] = turned(y_side[c], -8 * c)
                out[child, Z_ROWS] = z_side[c]
            return carry

        lax.fori_loop(0, 4, pair, 0)


def own_pieces(state, flags, owners):
    fields = state.shape[0]
    return pl.pallas_call(
        own_kernel,
        out_shape=[
            jax.ShapeDtypeStruct((KIDS, ROWS, LANES), F32),
            jax.ShapeDtypeStruct((3 * PARENTS + KIDS,), jnp.int32),
        ],
        in_specs=[ANY, pl.BlockSpec(memory_space=pltpu.VMEM), SMEM],
        out_specs=[pl.BlockSpec(memory_space=pltpu.VMEM), SMEM],
        scratch_shapes=[
            pltpu.VMEM((PARENTS, 2, fields, BS + 1, 24, LANES), F32),
            pltpu.VMEM((fields * PITCH, LANES), F32),
            pltpu.SemaphoreType.DMA((PARENTS, 2, fields)),
        ],
        compiler_params=pltpu.CompilerParams(vmem_limit_bytes=50 * MIB),
        cost_estimate=pl.CostEstimate(
            flops=10**7, bytes_accessed=20 * 10**6, transcendentals=0
        ),
        name="own_pieces",
    )(state, flags, owners)


def corner_kernel(col_even, col_odd, cor_even, cor_odd, sems):
    nx = col_even.shape[1]
    high_in_even = parity("rows") == 0
    copies = []
    for number, (ref, high) in enumerate(
        ((cor_even, high_in_even), (cor_odd, jnp.logical_not(high_in_even)))
    ):
        at = pl.ds(pl.multiple_of(jnp.where(high, nx - 8, 0), 8), 8)
        for half, source in enumerate((col_even, col_odd)):
            copies.append(
                pltpu.make_async_copy(source.at[:, at], ref.at[half], sems.at[number, half])
            )
    for c in copies:
        c.start()
    for c in copies:
        c.wait()


def pack_corners(col_even, col_odd):
    layers, _, nz = col_even.shape
    corner = jax.ShapeDtypeStruct((2, layers, 8, nz), F32)
    return pl.pallas_call(
        corner_kernel,
        out_shape=[corner, corner],
        in_specs=[ANY] * 2,
        out_specs=[pl.BlockSpec(memory_space=pltpu.VMEM)] * 2,
        scratch_shapes=[pltpu.SemaphoreType.DMA((2, 2))],
        compiler_params=pltpu.CompilerParams(vmem_limit_bytes=8 * MIB),
        name="pack_corners",
    )(col_even, col_odd)


def finish_kernel(
    info, own, row_even, row_odd, col_even, col_odd, out, beside_x, beside_y, kid_sems, sems
):
    nk = row_even.shape[2] // LANES
    nx = col_even.shape[1]
    row_par, col_par = parity("rows"), parity("cols")
    waits = []
    for r in range(PARENTS):
        ix, iy, kz = info[3 * r], info[3 * r + 1], info[3 * r + 2]
        columns, shift = z_place(kz, nk)
        for t in range(2):

            def row_copy(source):
                return pltpu.make_async_copy(
                    source.at[pl.ds(0, 8), pl.ds(pl.multiple_of(iy * BS, BS), BS), columns[t]],
                    beside_x.at[r, t],
                    sems.at[r, t, 0],
                )

            def col_copy(source):
                return pltpu.make_async_copy(
                    source.at[pl.ds(0, 8), pl.ds(pl.multiple_of(ix * BS, BS), BS), columns[t]],
                    beside_y.at[r, t],
                    sems.at[r, t, 1],
                )

            @pl.when(ix != row_par)
            def _():
                row_copy(row_even).start()

            @pl.when(ix == row_par)
            def _():
                row_copy(row_odd).start()

            @pl.when(iy != col_par)
            def _():
                col_copy(col_even).start()

            @pl.when(iy == col_par)
            def _():
                col_copy(col_odd).start()

            waits += [row_copy(row_even), col_copy(col_even)]
    out[...] = jnp.zeros_like(out)
    kid_copies = [
        pltpu.make_async_copy(own.at[n], out.at[info[3 * PARENTS + n]], kid_sems.at[n])
        for n in range(KIDS)
    ]
    for c in kid_copies:
        c.start()
    for c in waits + kid_copies:
        c.wait()

    lane = lax.broadcasted_iota(jnp.int32, (8, LANES), 1)
    sub = lax.broadcasted_iota(jnp.int32, (8, LANES), 0)
    zero = jnp.zeros((8, LANES), F32)
    for r in range(PARENTS):
        ix, iy, kz = info[3 * r], info[3 * r + 1], info[3 * r + 2]
        _, shift = z_place(kz, nk)
        from_first = lane >= shift

        def cell(source, n):
            halves = [flat_rows(source.at[r, t])[pl.ds(n, 8, stride=BS), :] for t in range(2)]
            value = jnp.where(from_first, halves[0], halves[1])
            return jnp.where((sub == 0) & (value == 0.0), 1.0, value)

        first_kid = 3 * PARENTS + 8 * r
        here = (lane < 64) == (ix == 1)
        for b in range(2):
            sums = [zero, zero]
            for j in range(8):
                moved = to_lane(cell(beside_x, 8 * b + j), 8 * j - 1 - shift)
                for c in range(2):
                    sums[c] = jnp.where(lanes_from(lane, 8 * j + 8 * c, 8), moved, sums[c])
            for c in range(2):
                slot = info[first_kid + 4 * ix + 2 * b + c]
                value = to_lane(sums[c], 64 * (1 - ix) - 8 * c)
                out[slot, X_ROWS] = jnp.where(here, value, out[slot, X_ROWS])

        here = (lane // 8) % 2 == iy
        for a in range(2):
            sums = [zero, zero]
            for i in range(8):
                first = 64 * (i % 2) + 16 * (i // 2)
                moved = to_lane(cell(beside_y, 8 * a + i), first - 1 - shift)
                for c in range(2):
                    sums[c] = jnp.where(lanes_from(lane, first + 8 * c, 8), moved, sums[c])
            for c in range(2):
                slot = info[first_kid + 4 * a + 2 * iy + c]
                value = to_lane(sums[c], 8 * iy - 8 * c)
                out[slot, Y_ROWS] = jnp.where(here, value, out[slot, Y_ROWS])


def finish_pieces(info, own, rows_halo, cols_halo, count):
    return pl.pallas_call(
        finish_kernel,
        out_shape=jax.ShapeDtypeStruct((count * CAP, ROWS, LANES), F32),
        in_specs=[SMEM] + [ANY] * 5,
        out_specs=pl.BlockSpec(memory_space=pltpu.VMEM),
        scratch_shapes=[
            pltpu.VMEM((PARENTS, 2, 8, BS, LANES), F32),
            pltpu.VMEM((PARENTS, 2, 8, BS, LANES), F32),
            pltpu.SemaphoreType.DMA((KIDS,)),
            pltpu.SemaphoreType.DMA((PARENTS, 2, 2)),
        ],
        compiler_params=pltpu.CompilerParams(vmem_limit_bytes=8 * MIB),
        name="finish_pieces",
    )(info, own, *rows_halo, *cols_halo)


def spread_weights():
    spread = np.zeros((3, LANES, 512), np.float32)
    for half in range(2):
        for y in range(BS):
            for z in range(BS):
                at = half * 64 + y // 2 * 8 + z // 2
                to = half * 256 + y * BS + z
                spread[0, at, to] = 1.0
                spread[1, at, to] = 0.25 * (2 * (y % 2) - 1)
                spread[2, at, to] = 0.25 * (2 * (z % 2) - 1)
    return spread


def limited(left, right):
    return jnp.maximum(jnp.minimum(left, right), 0.0) + jnp.minimum(jnp.maximum(left, right), 0.0)


def halves_of(value):
    top = value.astype(BF16)
    return top, (value - top.astype(F32)).astype(BF16)


def prolong_kernel(weights, piece, out, staged):
    count = piece.shape[0]
    sub = lax.broadcasted_iota(jnp.int32, (8, LANES), 0)
    lane = lax.broadcasted_iota(jnp.int32, (8, LANES), 1)
    cells = sub < 5

    def slopes(s, carry):
        for q in range(4):
            one_set(s, q)
        return carry

    def one_set(s, q):
        here = piece[s, 8 * q : 8 * q + 8]
        after = piece[s, 8 * q + 8 : 8 * q + 16] if q < 3 else piece[s, X_ROWS]
        prior = piece[s, 8 * q - 8 : 8 * q] if q else piece[s, X_ROWS]
        rows, points = piece[s, Y_ROWS], piece[s, Z_ROWS]
        x_up = turned(jnp.where(lane < 64, after, here), 64) - here
        x_down = here - turned(jnp.where(lane < 64, here, prior), 64)
        y_up = jnp.where(lane % 64 >= 56, turned(rows, 48 - 16 * q), turned(here, -8)) - here
        y_down = here - jnp.where(lane % 64 < 8, turned(rows, -16 * q), turned(here, 8))
        z_up = jnp.where(lane % 8 == 7, turned(points, 6 - 2 * q), turned(here, -1)) - here
        z_down = here - jnp.where(lane % 8 == 0, turned(points, -2 * q), turned(here, 1))
        slope_x = jnp.where(cells, limited(x_up, x_down), jnp.where(sub == 5, x_up, 0.0))
        slope_y = jnp.where(cells, limited(y_up, y_down), jnp.where(sub == 6, y_up, 0.0))
        slope_z = jnp.where(cells, limited(z_up, z_down), jnp.where(sub == 7, z_up, 0.0))
        middle = here + jnp.where(cells, 0.0, 0.25 * (slope_x + slope_y + slope_z))
        at = pl.ds(pl.multiple_of(s * 32, 32) + 8 * q, 8)
        step = 0.25 * slope_x
        staged[0, at] = middle - step
        staged[1, at] = middle + step
        staged[2, at] = slope_y
        staged[3, at] = slope_z

    lax.fori_loop(0, count, slopes, 0)

    def dot(parts, matrix):
        halves = [halves_of(staged[n]) for n in parts]
        value = jnp.concatenate([h[0] for h in halves] + [h[1] for h in halves], axis=1)
        return jnp.dot(value, matrix, preferred_element_type=F32)

    tilt = dot((2, 3), weights[2 * LANES :])
    for p in range(2):
        fine = dot((p,), weights[0 : 2 * LANES]) + tilt
        for s in range(count):
            for i in range(8):
                x = 2 * i + p
                at = s * 32 + 8 * (i // 2)
                out[0, 0, s // 2, s % 2, :, x * 256 : (x + 1) * 256] = fine[
                    at : at + 8, 256 * (i % 2) : 256 * (i % 2) + 256
                ]


def prolong(received, count):
    group = 8
    weights = spread_weights()
    stacked = np.concatenate([weights[n] for n in (0, 0, 1, 2, 1, 2)])
    return pl.pallas_call(
        prolong_kernel,
        grid=(count * CAP // group,),
        out_shape=jax.ShapeDtypeStruct((1, 1, count, CAP, 8, BS**3), F32),
        in_specs=[
            pl.BlockSpec(stacked.shape, lambda g: (0, 0)),
            pl.BlockSpec((group, ROWS, LANES), lambda g: (g, 0, 0)),
        ],
        out_specs=pl.BlockSpec(
            (1, 1, group // CAP, CAP, 8, BS**3), lambda g: (0, 0, g, 0, 0, 0)
        ),
        scratch_shapes=[pltpu.VMEM((4, group * 32, LANES), F32)],
        compiler_params=pltpu.CompilerParams(vmem_limit_bytes=16 * MIB),
        name="prolong",
    )(jnp.asarray(stacked, BF16), received)


def on_device(state, flags, owners):
    rows, cols = lax.axis_size("rows"), lax.axis_size("cols")
    row_even, row_odd, col_even, col_odd = pack(state)
    col_even = lax.ppermute(col_even, "cols", even_swap(cols))
    col_odd = lax.ppermute(col_odd, "cols", odd_swap(cols))
    row_even = lax.ppermute(row_even, "rows", even_swap(rows))
    row_odd = lax.ppermute(row_odd, "rows", odd_swap(rows))
    own, info = own_pieces(state, flags, owners)
    own, row_even, row_odd, col_even, col_odd = lax.optimization_barrier(
        (own, row_even, row_odd, col_even, col_odd)
    )
    rows_halo, cols_halo = (row_even, row_odd), (col_even, col_odd)
    cor_even, cor_odd = pack_corners(col_even, col_odd)
    cor_even = lax.ppermute(cor_even, "rows", even_swap(rows))
    cor_odd = lax.ppermute(cor_odd, "rows", odd_swap(rows))
    sent = finish_pieces(info, own, rows_halo, cols_halo, cols)
    sent, cor_even, cor_odd = lax.optimization_barrier((sent, cor_even, cor_odd))
    received = lax.all_to_all(
        sent.reshape((cols, CAP) + sent.shape[1:]), "cols", split_axis=0, concat_axis=0, tiled=True
    )
    faces_new = advance(state, rows_halo, cols_halo, (cor_even, cor_odd))
    arrivals = prolong(received.reshape(sent.shape), cols)
    return faces_new, arrivals


def solution(mesh):
    return jax.shard_map(
        on_device,
        mesh=mesh,
        in_specs=(
            P(None, "rows", "cols", None),
            P("rows", "cols", None),
            P(("rows", "cols"), None),
        ),
        out_specs=(P(None, "rows", "cols", None), P("rows", "cols", None, None, None, None)),
        check_vma=False,
    )
```

time: 89.5 us -> 71.7 us (0.80)
  the two profiles are of different devices: /device:TPU:1 before, /device:TPU:8 now
where the time goes in v2:
time: 71.7 us; the launch traced here: 71.3 us
  Pallas kernels  35.3 us (49%)
  starting transfers between devices  19.1 us (27%)
  waiting for transfers between devices  11.5 us (16%)
  local copies, waits for them, and re-layouts  4.56 us (6%)
  between operations  0.78 us (1%)
    pallas_call x1, Pallas kernels, advance(): pl.pallas_call(advance_kernel, out_shape=jax.ShapeDtypeStruct((3, nx, ny,...  12.2 us
    all_to_all x1, starting transfers between devices, on_device(): lax.all_to_all(sent.reshape((cols, CAP) + sent.shape[1:]), 'cols', split_...  12.2 us
    pallas_call x1, Pallas kernels, own_pieces(): pl.pallas_call(own_kernel, out_shape=[jax.ShapeDtypeStruct((KIDS, ROWS, L...  7.23 us
    ppermute x1, waiting for transfers between devices, on_device(): col_even = lax.ppermute(col_even, 'cols', even_swap(cols))  6.52 us
    pallas_call x1, Pallas kernels, prolong(): pl.pallas_call(prolong_kernel, grid=(count * CAP // group,), out_shape=ja...  6.46 us
    pallas_call x1, Pallas kernels, pack(): pl.pallas_call(pack_kernel, out_shape=[row_shape, row_shape, col_shape, c...  6.39 us
    unnamed x15, local copies, waits for them, and re-layouts  4.56 us
    pallas_call x1, Pallas kernels, finish_pieces(): pl.pallas_call(finish_kernel, out_shape=jax.ShapeDtypeStruct((count * CAP...  2.88 us
  transfers between devices with their start and end apart: 7, of which 3 were waited for; matrix products, arithmetic and copies ran while one was open for 0% of the time, Pallas kernels for 31%

profile of v2, /device:TPU:8, one launch (start us, length us, event | category | flops | bytes accessed | tf_op | source)
XLA Modules:
  0.0 71.3 jit_solution(12767395948563376998)
XLA Ops:
  0.6 0.0 copy-start.6
  0.6 0.0 copy-start.5
  0.6 6.4 %pack.1 = (f32[9,32,512]{2,1,0:T(8,128)}, f32[9,32,512]{2,1,0:T(8,128)}, f32[9,32,512]{2,1,0:T(8,128)}, f32[9,32,512]{2,1,0:T(8,128)S(1)}) custom-call(f32[8,32,32,512]{3,2,1,0:T(8,128)} %state.5), custom_call_target="tpu_custom_call" | custom-call | tf_op jit(solution)/shard_map/pack/pallas_call | solution.py:106
  7.0 0.1 collective-permute-start
  7.1 2.4 %collective-permute-start.1 = (f32[9,32,512]{2,1,0:T(8,128)}, f32[9,32,512]{2,1,0:T(8,128)S(1)}, u32[]{:S(2)}, u32[]{:S(2)}) collective-permute-start(f32[9,32,512]{2,1,0:T(8,128)} %get-tuple-element.20), channel_id=1, source_target_pairs={{16,32},{32,16},{48,64},{64,48},{80,96},{96,80},{17,33},{33,17},{4... | collective-permute-start | bytes 1769480 | tf_op jit(solution)/shard_map/ppermute | solution.py:836
  9.5 1.7 %collective-permute-start.2 = (f32[9,32,512]{2,1,0:T(8,128)}, f32[9,32,512]{2,1,0:T(8,128)S(1)}, u32[]{:S(2)}, u32[]{:S(2)}) collective-permute-start(f32[9,32,512]{2,1,0:T(8,128)} %get-tuple-element.21), channel_id=1, source_target_pairs={{0,1},{1,0},{2,3},{3,2},{4,5},{5,4},{6,7},{7,6},{8,9},{9,8},{10,11... | collective-permute-start | bytes 1769480 | tf_op jit(solution)/shard_map/ppermute | solution.py:833
  11.2 0.7 collective-permute-start.3
  11.9 0.0 copy-done.6
  11.9 0.1 copy.6.owners
  11.9 0.0 copy-done.5
  12.0 7.2 %own_pieces.1 = (f32[16,56,128]{2,1,0:T(8,128)S(1)}, s32[22]{0:T(128)S(1)}) custom-call(f32[8,32,32,512]{3,2,1,0:T(8,128)} %state.5, s32[2,2,32]{2,1,0:T(2,128)S(1)} %copy-done.5, s32[16,1]{1,0:T(8,128)S(1)} %copy.6.owners), custom_call_target="tpu_custom_call" | custom-call | flops 10000000 | bytes 20000000 | tf_op jit(solution)/shard_map/own_pieces/pallas_call | solution.py:572
  19.2 0.0 collective-permute-done.row_even
  19.2 0.0 collective-permute-done.1.row_odd
  19.2 6.5 %collective-permute-done.2.col_even = f32[9,32,512]{2,1,0:T(8,128)S(1)} collective-permute-done((f32[9,32,512]{2,1,0:T(8,128)}, f32[9,32,512]{2,1,0:T(8,128)S(1)}, u32[]{:S(2)}, u32[]{:S(2)}) %collective-permute-start.2) | collective-permute-done | bytes 589856 | tf_op jit(solution)/shard_map/ppermute | solution.py:833
  25.7 0.0 collective-permute-done.3.col_odd
  25.7 0.1 pack_corners.1
  25.9 0.2 collective-permute-start.4
  26.1 1.9 %collective-permute-start.5 = (f32[2,9,8,512]{3,2,1,0:T(8,128)S(1)}, f32[2,9,8,512]{3,2,1,0:T(8,128)S(1)}, u32[]{:S(2)}, u32[]{:S(2)}) collective-permute-start(f32[2,9,8,512]{3,2,1,0:T(8,128)S(1)} %get-tuple-element.30), channel_id=1, source_target_pairs={{16,32},{32,16},{48,64},{64,48},{80,96},{96,80},{17,33},{33,17},{4... | collective-permute-start | bytes 884744 | tf_op jit(solution)/shard_map/ppermute | solution.py:844
  28.0 2.9 %finish_pieces.1 = f32[32,56,128]{2,1,0:T(8,128)} custom-call(s32[22]{0:T(128)S(1)} %get-tuple-element.27.info, f32[16,56,128]{2,1,0:T(8,128)S(1)} %get-tuple-element.28.own, f32[9,32,512]{2,1,0:T(8,128)S(1)} %collective-permute-done.row_even, f32[9,32,512]{2,1,0:T(8,128)S(1)} %collective-permute-done.1.row_odd, ...), custom_call_target="tpu_custom_call" | custom-call | tf_op jit(solution)/shard_map/finish_pieces/pallas_call | solution.py:719
  30.9 0.0 collective-permute-done.4.cor_even
  30.9 0.0 copy-start.1
  30.9 0.7 copy-done.1
  31.6 2.5 %collective-permute-done.5.cor_odd = f32[2,9,8,512]{3,2,1,0:T(8,128)S(1)} collective-permute-done((f32[2,9,8,512]{3,2,1,0:T(8,128)S(1)}, f32[2,9,8,512]{3,2,1,0:T(8,128)S(1)}, u32[]{:S(2)}, u32[]{:S(2)}) %collective-permute-start.5) | collective-permute-done | bytes 294944 | tf_op jit(solution)/shard_map/ppermute | solution.py:844
  34.1 0.7 copy-done.3
  34.8 12.2 %all-to-all-start = ((f32[16,2,56,128]{3,2,1,0:T(8,128)}), f32[16,2,56,128]{3,2,1,0:T(8,128)S(1)}, u32[]{:S(2)}, u32[]{:S(2)}) async-start(f32[16,2,56,128]{3,2,1,0:T(8,128)} %bitcast), calls=%async_computation | async-start | bytes 1835008 | tf_op jit(solution)/shard_map/all_to_all | solution.py:847
  47.0 0.0 copy-start.2
  47.0 1.0 %copy-done.2 = f32[2,9,8,512]{3,2,1,0:T(8,128)S(1)} copy-done((f32[2,9,8,512]{3,2,1,0:T(8,128)S(1)}, f32[2,9,8,512]{3,2,1,0:T(8,128)}, u32[]{:S(2)}) %copy-start.2) | copy-done | bytes 294936
  48.0 1.0 %copy-done.4 = f32[2,9,8,512]{3,2,1,0:T(8,128)S(1)} copy-done((f32[2,9,8,512]{3,2,1,0:T(8,128)S(1)}, f32[2,9,8,512]{3,2,1,0:T(8,128)}, u32[]{:S(2)}) %copy-start.4) | copy-done | bytes 294936
  49.0 12.2 %advance.1 = f32[3,32,32,512]{3,2,1,0:T(8,128)} custom-call(f32[8,32,32,512]{3,2,1,0:T(8,128)} %state.5, f32[9,32,512]{2,1,0:T(8,128)S(1)} %collective-permute-done.row_even, f32[9,32,512]{2,1,0:T(8,128)S(1)} %collective-permute-done.1.row_odd, f32[9,32,512]{2,1,0:T(8,128)S(1)} %collective-permute-done.2.col_even, ...), custom_call_target="tpu_custom_call" | custom-call | flops 31457280 | bytes 20971520 | tf_op jit(solution)/shard_map/advance/pallas_call | solution.py:363
  61.2 2.5 %all-to-all-done = f32[16,2,56,128]{3,2,1,0:T(8,128)S(1)} async-done(((f32[16,2,56,128]{3,2,1,0:T(8,128)}), f32[16,2,56,128]{3,2,1,0:T(8,128)S(1)}, u32[]{:S(2)}, u32[]{:S(2)}) %all-to-all-start) | async-done | bytes 917536 | tf_op jit(solution)/shard_map/all_to_all | solution.py:847
  63.7 1.1 %copy-done = bf16[768,512]{1,0:T(8,128)(2,1)S(1)} copy-done((bf16[768,512]{1,0:T(8,128)(2,1)S(1)}, bf16[768,512]{1,0:T(8,128)(2,1)}, u32[]{:S(2)}) %copy-start) | copy-done | bytes 786456
  64.8 6.5 %prolong.1 = f32[1,1,16,2,8,4096]{5,4,3,2,1,0:T(8,128)} custom-call(bf16[768,512]{1,0:T(8,128)(2,1)S(1)} %copy-done, f32[32,56,128]{2,1,0:T(8,128)S(1)} %bitcast.2), custom_call_target="tpu_custom_call" | custom-call | tf_op jit(solution)/shard_map/prolong/pallas_call | solution.py:813
  (3 shorter events, 0.0 us)
Async XLA Ops:
  0.6 11.2 %copy-start.6 = (s32[16,1]{0,1:T(1,128)S(1)}, s32[16,1]{0,1:T(1,128)}, u32[]{:S(2)}) copy-start(s32[16,1]{0,1:T(1,128)} %param.6) | copy-start | bytes 196
  0.6 11.3 %copy-start.5 = (s32[2,2,32]{2,1,0:T(2,128)S(1)}, s32[2,2,32]{2,1,0:T(2,128)}, u32[]{:S(2)}) copy-start(s32[2,2,32]{2,1,0:T(2,128)} %flags.1) | copy-start | bytes 1540
  7.0 12.2 %collective-permute-start = (f32[9,32,512]{2,1,0:T(8,128)}, f32[9,32,512]{2,1,0:T(8,128)S(1)}, u32[]{:S(2)}, u32[]{:S(2)}) collective-permute-start(f32[9,32,512]{2,1,0:T(8,128)} %get-tuple-element.19), channel_id=1, source_target_pairs={{0,16},{16,0},{32,48},{48,32},{64,80},{80,64},{96,112},{112,96},{1... | collective-permute-start | bytes 1769480 | tf_op jit(solution)/shard_map/ppermute | solution.py:835
  7.1 12.1 %collective-permute-start.1 = (f32[9,32,512]{2,1,0:T(8,128)}, f32[9,32,512]{2,1,0:T(8,128)S(1)}, u32[]{:S(2)}, u32[]{:S(2)}) collective-permute-start(f32[9,32,512]{2,1,0:T(8,128)} %get-tuple-element.20), channel_id=1, source_target_pairs={{16,32},{32,16},{48,64},{64,48},{80,96},{96,80},{17,33},{33,17},{4... | collective-permute-start | bytes 1769480 | tf_op jit(solution)/shard_map/ppermute | solution.py:836
  9.5 16.2 %collective-permute-start.2 = (f32[9,32,512]{2,1,0:T(8,128)}, f32[9,32,512]{2,1,0:T(8,128)S(1)}, u32[]{:S(2)}, u32[]{:S(2)}) collective-permute-start(f32[9,32,512]{2,1,0:T(8,128)} %get-tuple-element.21), channel_id=1, source_target_pairs={{0,1},{1,0},{2,3},{3,2},{4,5},{5,4},{6,7},{7,6},{8,9},{9,8},{10,11... | collective-permute-start | bytes 1769480 | tf_op jit(solution)/shard_map/ppermute | solution.py:833
  11.2 14.6 %collective-permute-start.3 = (f32[9,32,512]{2,1,0:T(8,128)S(1)}, f32[9,32,512]{2,1,0:T(8,128)S(1)}, u32[]{:S(2)}, u32[]{:S(2)}) collective-permute-start(f32[9,32,512]{2,1,0:T(8,128)S(1)} %get-tuple-element.22), channel_id=1, source_target_pairs={{1,2},{2,1},{3,4},{4,3},{5,6},{6,5},{7,8},{8,7},{9,10},{10,9},{11,... | collective-permute-start | bytes 1769480 | tf_op jit(solution)/shard_map/ppermute | solution.py:834
  25.9 5.0 %collective-permute-start.4 = (f32[2,9,8,512]{3,2,1,0:T(8,128)S(1)}, f32[2,9,8,512]{3,2,1,0:T(8,128)S(1)}, u32[]{:S(2)}, u32[]{:S(2)}) collective-permute-start(f32[2,9,8,512]{3,2,1,0:T(8,128)S(1)} %get-tuple-element.29), channel_id=1, source_target_pairs={{0,16},{16,0},{32,48},{48,32},{64,80},{80,64},{96,112},{112,96},{1... | collective-permute-start | bytes 884744 | tf_op jit(solution)/shard_map/ppermute | solution.py:843
  26.1 8.0 %collective-permute-start.5 = (f32[2,9,8,512]{3,2,1,0:T(8,128)S(1)}, f32[2,9,8,512]{3,2,1,0:T(8,128)S(1)}, u32[]{:S(2)}, u32[]{:S(2)}) collective-permute-start(f32[2,9,8,512]{3,2,1,0:T(8,128)S(1)} %get-tuple-element.30), channel_id=1, source_target_pairs={{16,32},{32,16},{48,64},{64,48},{80,96},{96,80},{17,33},{33,17},{4... | collective-permute-start | bytes 884744 | tf_op jit(solution)/shard_map/ppermute | solution.py:844
  30.9 0.7 %copy-start.1 = (f32[2,9,8,512]{3,2,1,0:T(8,128)}, f32[2,9,8,512]{3,2,1,0:T(8,128)S(1)}, u32[]{:S(2)}) copy-start(f32[2,9,8,512]{3,2,1,0:T(8,128)S(1)} %collective-permute-done.4.cor_even) | copy-start | bytes 884740
  34.1 0.7 copy-start.3
  34.8 28.9 %all-to-all-start = ((f32[16,2,56,128]{3,2,1,0:T(8,128)}), f32[16,2,56,128]{3,2,1,0:T(8,128)S(1)}, u32[]{:S(2)}, u32[]{:S(2)}) async-start(f32[16,2,56,128]{3,2,1,0:T(8,128)} %bitcast), calls=%async_computation | async-start | bytes 1835008 | tf_op jit(solution)/shard_map/all_to_all | solution.py:847
  47.0 1.0 %copy-start.2 = (f32[2,9,8,512]{3,2,1,0:T(8,128)S(1)}, f32[2,9,8,512]{3,2,1,0:T(8,128)}, u32[]{:S(2)}) copy-start(f32[2,9,8,512]{3,2,1,0:T(8,128)} %copy-done.1) | copy-start | bytes 884740
  48.0 1.0 %copy-start.4 = (f32[2,9,8,512]{3,2,1,0:T(8,128)S(1)}, f32[2,9,8,512]{3,2,1,0:T(8,128)}, u32[]{:S(2)}) copy-start(f32[2,9,8,512]{3,2,1,0:T(8,128)} %copy-done.3) | copy-start | bytes 884740
  63.7 1.1 %copy-start = (bf16[768,512]{1,0:T(8,128)(2,1)S(1)}, bf16[768,512]{1,0:T(8,128)(2,1)}, u32[]{:S(2)}) copy-start(bf16[768,512]{1,0:T(8,128)(2,1)} %constant.2.clone.weights) | copy-start | bytes 2359300

commit v3 on v2

--- a/solution.py
+++ b/solution.py
@@ -42,7 +42,7 @@
     return lax.rem(lax.axis_index(axis), 2)
 
 
-def pack_kernel(state, row_even, row_odd, col_even, col_odd, tiles, rims, row_sems, sems, out_sems):
+def pack_kernel(state, col_even, col_odd, token, tiles, rims, sems, out_sems):
     nx, ny = state.shape[1], state.shape[2]
     nk = state.shape[3] // LANES
 
@@ -57,19 +57,6 @@
         for side in range(2):
             for f in range(0, 8, 2):
                 tile_in(side, k, f).start()
-    at_even = jnp.where(parity("rows") == 0, nx - 1, 0)
-    at_odd = nx - 1 - at_even
-    row_copies = []
-    for number, (ref, at) in enumerate(((row_even, at_even), (row_odd, at_odd))):
-        second = jnp.where(at == 0, 1, nx - 2)
-        row_copies.append(
-            pltpu.make_async_copy(state.at[:, at], ref.at[pl.ds(0, 8)], row_sems.at[number, 0])
-        )
-        row_copies.append(
-            pltpu.make_async_copy(state.at[5, second], ref.at[8], row_sems.at[number, 1])
-        )
-    for c in row_copies:
-        c.start()
     high_in_even = parity("cols") == 0
     outs = []
     for k in range(nk):
@@ -94,24 +81,23 @@
             )
             c.start()
             outs.append(c)
-    for c in row_copies + outs:
+    token[0] = 0
+    for c in outs:
         c.wait()
 
 
 def pack(state):
     fields, nx, ny, nz = state.shape
     nk = nz // LANES
-    row_shape = jax.ShapeDtypeStruct((fields + 1, ny, nz), F32)
     col_shape = jax.ShapeDtypeStruct((fields + 1, nx, nz), F32)
     return pl.pallas_call(
         pack_kernel,
-        out_shape=[row_shape, row_shape, col_shape, col_shape],
+        out_shape=[col_shape, col_shape, jax.ShapeDtypeStruct((1,), jnp.int32)],
         in_specs=[ANY],
-        out_specs=[pl.BlockSpec(memory_space=pltpu.VMEM)] * 2 + [ANY] * 2,
+        out_specs=[ANY, ANY, SMEM],
         scratch_shapes=[
             pltpu.VMEM((2, nk, fields, nx, 8, LANES), F32),
             pltpu.VMEM((2, nk, fields + 1, nx, LANES), F32),
-            pltpu.SemaphoreType.DMA((2, 2)),
             pltpu.SemaphoreType.DMA((2, nk, fields)),
             pltpu.SemaphoreType.DMA((2, nk)),
         ],
@@ -141,7 +127,7 @@
 
 def advance_kernel(
     state, row_even, row_odd, col_even, col_odd, cor_even, cor_odd,
-    out, dens, flds, rims, rim_e, edge, prev, done, in_sems, halo_sems, out_sems,
+    out, dens, flds, rims, ends, rim_e, edge, prev, done, in_sems, halo_sems, out_sems,
 ):
     nx, ny, nz = state.shape[1:]
     nk = nz // LANES
@@ -178,11 +164,12 @@
     def cols_in(source, side):
         return [pltpu.make_async_copy(source, rims.at[side, :, pl.ds(8, nx)], halo_sems.at[side, 3])]
 
-    def corner_in(source, half, side, end):
-        to = pl.ds(0 if end == 0 else nx + 8, 8)
-        return [
-            pltpu.make_async_copy(source.at[half], rims.at[side, :, to], halo_sems.at[side, 4 + end])
-        ]
+    corner_copies = [
+        pltpu.make_async_copy(source, ends.at[n], halo_sems.at[n, 4])
+        for n, source in enumerate((cor_even, cor_odd))
+    ]
+    for c in corner_copies:
+        c.start()
 
     for side in range(2):
         @pl.when(row_par == side)
@@ -205,18 +192,6 @@
             for c in cols_in(col_even, side):
                 c.start()
 
-        half = jnp.where(col_par == side, 1, 0)
-        for end in range(2):
-            @pl.when(row_par == end)
-            def _():
-                for c in corner_in(cor_odd, half, side, end):
-                    c.start()
-
-            @pl.when(row_par != end)
-            def _():
-                for c in corner_in(cor_even, half, side, end):
-                    c.start()
-
     for c in range(ahead):
         for copy in chunk_in(c):
             copy.start()
@@ -224,9 +199,19 @@
     for side in range(2):
         for c in rows_in(row_even, side) + cols_in(col_even, side):
             c.wait()
+
+    for c in corner_copies:
+        c.wait()
+    for side in range(2):
         for end in range(2):
-            for c in corner_in(cor_even, 0, side, end):
-                c.wait()
+            row_swap = jnp.where(row_par == end, 1, 0)
+            col_swap = jnp.where(col_par == side, 1, 0)
+            at = 7 if end == 0 else nx + 8
+            for f in range(8):
+                rims[side, f, at : at + 1] = ends[row_swap, col_swap, f : f + 1]
+            rims[side, 8, at : at + 1] = ends[row_swap, col_swap, 9:10]
+            if end == 1:
+                rims[side, 5, at + 1 : at + 2] = ends[row_swap, col_swap, 8:9]
 
     for at in (0, nx + 1):
         dens[at] = jnp.where(dens[at] > 0.0, dens[at], 1.0)
@@ -369,6 +354,7 @@
             pltpu.VMEM((nx + 2, ny, nz), F32),
             pltpu.VMEM((6, nx + 3, ny, nz), F32),
             pltpu.VMEM((2, 9, nx + 16, nz), F32),
+            pltpu.VMEM((2, 2, 16, nz), F32),
             pltpu.VMEM((4, 2, nk, nx + 16, LANES), F32),
             pltpu.VMEM((3, nk, ny + 16, LANES), F32),
             pltpu.VMEM((5, nk, ny, LANES), F32),
@@ -428,7 +414,10 @@
     return jnp.where(here & (at == 2 * quarter + 1), high, side)
 
 
-def own_kernel(state, flags, owners, out, info, window, aligned, sems):
+def own_kernel(
+    token, state, flags, owners, out, info, row_even, row_odd,
+    window, aligned, sems, row_sems,
+):
     nx, ny, nz = state.shape[1:]
     nk = nz // LANES
     gx, gy, gz = flags.shape
@@ -467,6 +456,20 @@
                 c.start()
         spots.append((ix, iy, kz, shift, copies))
         info[3 * r], info[3 * r + 1], info[3 * r + 2] = ix, iy, kz
+
+    at_even = jnp.where(parity("rows") == 0, nx - 1, 0)
+    at_odd = nx - 1 - at_even
+    row_copies = []
+    for number, (ref, at) in enumerate(((row_even, at_even), (row_odd, at_odd))):
+        second = jnp.where(at == 0, 1, nx - 2)
+        row_copies.append(
+            pltpu.make_async_copy(state.at[:, at], ref.at[pl.ds(0, 8)], row_sems.at[number, 0])
+        )
+        row_copies.append(
+            pltpu.make_async_copy(state.at[5, second], ref.at[8], row_sems.at[number, 1])
+        )
+    for c in row_copies:
+        c.start()
 
     names = [owners[n, 0] for n in range(KIDS)]
     for n in range(KIDS):
@@ -566,57 +569,78 @@
 
         lax.fori_loop(0, 4, pair, 0)
 
-
-def own_pieces(state, flags, owners):
-    fields = state.shape[0]
+    for c in row_copies:
+        c.wait()
+
+
+def own_pieces(token, state, flags, owners):
+    fields, _, ny, nz = state.shape
     return pl.pallas_call(
         own_kernel,
         out_shape=[
             jax.ShapeDtypeStruct((KIDS, ROWS, LANES), F32),
             jax.ShapeDtypeStruct((3 * PARENTS + KIDS,), jnp.int32),
-        ],
-        in_specs=[ANY, pl.BlockSpec(memory_space=pltpu.VMEM), SMEM],
-        out_specs=[pl.BlockSpec(memory_space=pltpu.VMEM), SMEM],
+        ]
+        + [jax.ShapeDtypeStruct((fields + 1, ny, nz), F32)] * 2,
+        in_specs=[SMEM, ANY, pl.BlockSpec(memory_space=pltpu.VMEM), SMEM],
+        out_specs=[pl.BlockSpec(memory_space=pltpu.VMEM), SMEM]
+        + [pl.BlockSpec(memory_space=pltpu.VMEM)] * 2,
         scratch_shapes=[
             pltpu.VMEM((PARENTS, 2, fields, BS + 1, 24, LANES), F32),
             pltpu.VMEM((fields * PITCH, LANES), F32),
             pltpu.SemaphoreType.DMA((PARENTS, 2, fields)),
+            pltpu.SemaphoreType.DMA((2, 2)),
         ],
         compiler_params=pltpu.CompilerParams(vmem_limit_bytes=50 * MIB),
         cost_estimate=pl.CostEstimate(
             flops=10**7, bytes_accessed=20 * 10**6, transcendentals=0
         ),
         name="own_pieces",
-    )(state, flags, owners)
-
-
-def corner_kernel(col_even, col_odd, cor_even, cor_odd, sems):
+    )(token, state, flags, owners)
+
+
+def corner_kernel(col_even, col_odd, cor_even, cor_odd, ends, sems):
     nx = col_even.shape[1]
-    high_in_even = parity("rows") == 0
+    nk = col_even.shape[2] // LANES
     copies = []
-    for number, (ref, high) in enumerate(
-        ((cor_even, high_in_even), (cor_odd, jnp.logical_not(high_in_even)))
-    ):
-        at = pl.ds(pl.multiple_of(jnp.where(high, nx - 8, 0), 8), 8)
-        for half, source in enumerate((col_even, col_odd)):
-            copies.append(
-                pltpu.make_async_copy(source.at[:, at], ref.at[half], sems.at[number, half])
-            )
+    for half, source in enumerate((col_even, col_odd)):
+        for end in range(2):
+            for k in range(nk):
+                copies.append(
+                    pltpu.make_async_copy(
+                        source.at[:, pl.ds(end * (nx - 8), 8), pl.ds(k * LANES, LANES)],
+                        ends.at[half, end, k],
+                        sems.at[half, end, k],
+                    )
+                )
     for c in copies:
         c.start()
     for c in copies:
         c.wait()
+    for number, ref in enumerate((cor_even, cor_odd)):
+        end = 1 - parity("rows") if number == 0 else parity("rows")
+        for half in range(2):
+            for k in range(nk):
+                cut = slice(k * LANES, (k + 1) * LANES)
+                flat = flat_rows(ends.at[half, end, k])
+                ref[half, 0:8, cut] = flat[pl.ds(7 * end, 8, stride=8), :]
+                ref[half, 8:16, cut] = jnp.zeros((8, LANES), F32)
+                ref[half, 8:9, cut] = flat[pl.ds(5 * 8 + 1 + 5 * end, 1), :]
+                ref[half, 9:10, cut] = flat[pl.ds(8 * 8 + 7 * end, 1), :]
 
 
 def pack_corners(col_even, col_odd):
     layers, _, nz = col_even.shape
-    corner = jax.ShapeDtypeStruct((2, layers, 8, nz), F32)
+    corner = jax.ShapeDtypeStruct((2, 16, nz), F32)
     return pl.pallas_call(
         corner_kernel,
         out_shape=[corner, corner],
         in_specs=[ANY] * 2,
         out_specs=[pl.BlockSpec(memory_space=pltpu.VMEM)] * 2,
-        scratch_shapes=[pltpu.SemaphoreType.DMA((2, 2))],
+        scratch_shapes=[
+            pltpu.VMEM((2, 2, nz // LANES, layers, 8, LANES), F32),
+            pltpu.SemaphoreType.DMA((2, 2, nz // LANES)),
+        ],
         compiler_params=pltpu.CompilerParams(vmem_limit_bytes=8 * MIB),
         name="pack_corners",
     )(col_even, col_odd)
@@ -829,19 +853,16 @@
 
 def on_device(state, flags, owners):
     rows, cols = lax.axis_size("rows"), lax.axis_size("cols")
-    row_even, row_odd, col_even, col_odd = pack(state)
+    col_even, col_odd, token = pack(state)
     col_even = lax.ppermute(col_even, "cols", even_swap(cols))
     col_odd = lax.ppermute(col_odd, "cols", odd_swap(cols))
+    own, info, row_even, row_odd = own_pieces(token, state, flags, owners)
     row_even = lax.ppermute(row_even, "rows", even_swap(rows))
     row_odd = lax.ppermute(row_odd, "rows", odd_swap(rows))
-    own, info = own_pieces(state, flags, owners)
-    own, row_even, row_odd, col_even, col_odd = lax.optimization_barrier(
-        (own, row_even, row_odd, col_even, col_odd)
-    )
-    rows_halo, cols_halo = (row_even, row_odd), (col_even, col_odd)
     cor_even, cor_odd = pack_corners(col_even, col_odd)
     cor_even = lax.ppermute(cor_even, "rows", even_swap(rows))
     cor_odd = lax.ppermute(cor_odd, "rows", odd_swap(rows))
+    rows_halo, cols_halo = (row_even, row_odd), (col_even, col_odd)
     sent = finish_pieces(info, own, rows_halo, cols_halo, cols)
     sent, cor_even, cor_odd = lax.optimization_barrier((sent, cor_even, cor_odd))
     received = lax.all_to_all(

time: 71.7 us -> 65.6 us (0.915)
  local copies, waits for them, and re-layouts: 4.56 us -> 1.23 us
  starting transfers between devices: 19.1 us -> 17.3 us
  waiting for transfers between devices: 11.5 us -> 10.4 us
    ppermute x1, waiting for transfers between devices: 6.52 us -> 2.51 us  [on_device(): col_even = lax.ppermute(col_even, 'cols', even_swap(cols))]
    ppermute x1, waiting for transfers between devices: 0.01 us -> 3.62 us  [on_device(): row_odd = lax.ppermute(row_odd, 'rows', odd_swap(rows))]
    unnamed x15 -> x7, local copies, waits for them, and re-layouts: 4.56 us -> 1.23 us
    ppermute x1, waiting for transfers between devices: 2.5 us -> 0.01 us  [on_device(): cor_odd = lax.ppermute(cor_odd, 'rows', odd_swap(rows))]
    all_to_all x1, starting transfers between devices: 12.2 us -> 10.2 us  [on_device(): lax.all_to_all(sent.reshape((cols, CAP) + sent.shape[1:]), 'cols', split_...]
    all_to_all x1, waiting for transfers between devices: 2.49 us -> 4.31 us  [on_device(): lax.all_to_all(sent.reshape((cols, CAP) + sent.shape[1:]), 'cols', split_...]
    pallas_call x1, Pallas kernels: 6.39 us -> 5.62 us  [pack(): pl.pallas_call(pack_kernel, out_shape=[col_shape, col_shape, jax.ShapeDty...]
  transfers between devices with their start and end apart: 7 -> 7, of which waited for: 3 -> 3; matrix products, arithmetic and copies ran while one was open for 0% -> 0% of each run, Pallas kernels for 31% -> 36%
where the time goes in v3:
time: 65.6 us; the launch traced here: 65.3 us
  Pallas kernels  35.5 us (54%)
  starting transfers between devices  17.3 us (26%)
  waiting for transfers between devices  10.4 us (16%)
  local copies, waits for them, and re-layouts  1.23 us (2%)
  between operations  0.77 us (1%)
    pallas_call x1, Pallas kernels, advance(): pl.pallas_call(advance_kernel, out_shape=jax.ShapeDtypeStruct((3, nx, ny,...  12.3 us
    all_to_all x1, starting transfers between devices, on_device(): lax.all_to_all(sent.reshape((cols, CAP) + sent.shape[1:]), 'cols', split_...  10.2 us
    pallas_call x1, Pallas kernels, own_pieces(): pl.pallas_call(own_kernel, out_shape=[jax.ShapeDtypeStruct((KIDS, ROWS, L...  7.93 us
    pallas_call x1, Pallas kernels, prolong(): pl.pallas_call(prolong_kernel, grid=(count * CAP // group,), out_shape=ja...  6.46 us
    pallas_call x1, Pallas kernels, pack(): pl.pallas_call(pack_kernel, out_shape=[col_shape, col_shape, jax.ShapeDty...  5.62 us
    all_to_all x1, waiting for transfers between devices, on_device(): lax.all_to_all(sent.reshape((cols, CAP) + sent.shape[1:]), 'cols', split_...  4.31 us
    ppermute x1, waiting for transfers between devices, on_device(): row_odd = lax.ppermute(row_odd, 'rows', odd_swap(rows))  3.62 us
    pallas_call x1, Pallas kernels, finish_pieces(): pl.pallas_call(finish_kernel, out_shape=jax.ShapeDtypeStruct((count * CAP...  2.88 us
  transfers between devices with their start and end apart: 7, of which 3 were waited for; matrix products, arithmetic and copies ran while one was open for 0% of the time, Pallas kernels for 36%

profile of v3, /device:TPU:8, one launch (start us, length us, event | category | flops | bytes accessed | tf_op | source)
XLA Modules:
  0.0 65.3 jit_solution(11448318965659226251)
XLA Ops:
  0.6 0.0 copy-start.2
  0.6 0.0 copy-start.1
  0.6 5.6 %pack.1 = (f32[9,32,512]{2,1,0:T(8,128)}, f32[9,32,512]{2,1,0:T(8,128)}, s32[1]{0:T(128)}) custom-call(f32[8,32,32,512]{3,2,1,0:T(8,128)} %state.5), custom_call_target="tpu_custom_call" | custom-call | tf_op jit(solution)/shard_map/pack/pallas_call | solution.py:93
  6.3 1.6 %collective-permute-start.2 = (f32[9,32,512]{2,1,0:T(8,128)}, f32[9,32,512]{2,1,0:T(8,128)S(1)}, u32[]{:S(2)}, u32[]{:S(2)}) collective-permute-start(f32[9,32,512]{2,1,0:T(8,128)} %get-tuple-element.17), channel_id=1, source_target_pairs={{0,1},{1,0},{2,3},{3,2},{4,5},{5,4},{6,7},{7,6},{8,9},{9,8},{10,11... | collective-permute-start | bytes 1769480 | tf_op jit(solution)/shard_map/ppermute | solution.py:857
  7.9 0.7 %collective-permute-start.3 = (f32[9,32,512]{2,1,0:T(8,128)}, f32[9,32,512]{2,1,0:T(8,128)S(1)}, u32[]{:S(2)}, u32[]{:S(2)}) collective-permute-start(f32[9,32,512]{2,1,0:T(8,128)} %get-tuple-element.18), channel_id=1, source_target_pairs={{1,2},{2,1},{3,4},{4,3},{5,6},{6,5},{7,8},{8,7},{9,10},{10,9},{11,... | collective-permute-start | bytes 1769480 | tf_op jit(solution)/shard_map/ppermute | solution.py:858
  8.5 0.0 copy-done.2
  8.6 0.1 copy.6.owners
  8.6 0.0 copy-done.1
  8.6 7.9 %own_pieces.1 = (f32[16,56,128]{2,1,0:T(8,128)S(1)}, s32[22]{0:T(128)S(1)}, f32[9,32,512]{2,1,0:T(8,128)S(1)}, f32[9,32,512]{2,1,0:T(8,128)S(1)}) custom-call(s32[1]{0:T(128)} %get-tuple-element.14.token, f32[8,32,32,512]{3,2,1,0:T(8,128)} %state.5, s32[2,2,32]{2,1,0:T(2,128)S(1)} %copy-done.1, s32[16,1]{1,0:T(8,128)S(1)} %copy.6.owners), custom_call_target="tpu_custom_call" | custom-call | flops 10000000 | bytes 20000000 | tf_op jit(solution)/shard_map/own_pieces/pallas_call | solution.py:578
  16.6 0.1 collective-permute-start
  16.7 2.4 %collective-permute-start.1 = (f32[9,32,512]{2,1,0:T(8,128)S(1)}, f32[9,32,512]{2,1,0:T(8,128)S(1)}, u32[]{:S(2)}, u32[]{:S(2)}) collective-permute-start(f32[9,32,512]{2,1,0:T(8,128)S(1)} %get-tuple-element.16), channel_id=1, source_target_pairs={{16,32},{32,16},{48,64},{64,48},{80,96},{96,80},{17,33},{33,17},{4... | collective-permute-start | bytes 1769480 | tf_op jit(solution)/shard_map/ppermute | solution.py:861
  19.1 2.5 %collective-permute-done.2.col_even = f32[9,32,512]{2,1,0:T(8,128)S(1)} collective-permute-done((f32[9,32,512]{2,1,0:T(8,128)}, f32[9,32,512]{2,1,0:T(8,128)S(1)}, u32[]{:S(2)}, u32[]{:S(2)}) %collective-permute-start.2) | collective-permute-done | bytes 589856 | tf_op jit(solution)/shard_map/ppermute | solution.py:857
  21.6 0.0 collective-permute-done.3.col_odd
  21.6 0.3 pack_corners.1
  21.9 0.1 collective-permute-start.4
  22.0 2.2 %collective-permute-start.5 = (f32[2,16,512]{2,1,0:T(8,128)S(1)}, f32[2,16,512]{2,1,0:T(8,128)S(1)}, u32[]{:S(2)}, u32[]{:S(2)}) collective-permute-start(f32[2,16,512]{2,1,0:T(8,128)S(1)} %get-tuple-element.22), channel_id=1, source_target_pairs={{16,32},{32,16},{48,64},{64,48},{80,96},{96,80},{17,33},{33,17},{4... | collective-permute-start | bytes 196616 | tf_op jit(solution)/shard_map/ppermute | solution.py:864
  24.2 0.0 collective-permute-done.row_even
  24.3 3.6 %collective-permute-done.1.row_odd = f32[9,32,512]{2,1,0:T(8,128)S(1)} collective-permute-done((f32[9,32,512]{2,1,0:T(8,128)S(1)}, f32[9,32,512]{2,1,0:T(8,128)S(1)}, u32[]{:S(2)}, u32[]{:S(2)}) %collective-permute-start.1) | collective-permute-done | bytes 589856 | tf_op jit(solution)/shard_map/ppermute | solution.py:861
  27.9 2.9 %finish_pieces.1 = f32[32,56,128]{2,1,0:T(8,128)} custom-call(s32[22]{0:T(128)S(1)} %get-tuple-element.19.info, f32[16,56,128]{2,1,0:T(8,128)S(1)} %get-tuple-element.20.own, f32[9,32,512]{2,1,0:T(8,128)S(1)} %collective-permute-done.row_even, f32[9,32,512]{2,1,0:T(8,128)S(1)} %collective-permute-done.1.row_odd, ...), custom_call_target="tpu_custom_call" | custom-call | tf_op jit(solution)/shard_map/finish_pieces/pallas_call | solution.py:743
  30.8 0.0 collective-permute-done.4.cor_even
  30.8 0.0 collective-permute-done.5.cor_odd
  30.8 10.2 %all-to-all-start = ((f32[16,2,56,128]{3,2,1,0:T(8,128)}), f32[16,2,56,128]{3,2,1,0:T(8,128)S(1)}, u32[]{:S(2)}, u32[]{:S(2)}) async-start(f32[16,2,56,128]{3,2,1,0:T(8,128)} %bitcast), calls=%async_computation | async-start | bytes 1835008 | tf_op jit(solution)/shard_map/all_to_all | solution.py:868
  41.0 12.3 %advance.1 = f32[3,32,32,512]{3,2,1,0:T(8,128)} custom-call(f32[8,32,32,512]{3,2,1,0:T(8,128)} %state.5, f32[9,32,512]{2,1,0:T(8,128)S(1)} %collective-permute-done.row_even, f32[9,32,512]{2,1,0:T(8,128)S(1)} %collective-permute-done.1.row_odd, f32[9,32,512]{2,1,0:T(8,128)S(1)} %collective-permute-done.2.col_even, ...), custom_call_target="tpu_custom_call" | custom-call | flops 31457280 | bytes 20971520 | tf_op jit(solution)/shard_map/advance/pallas_call | solution.py:348
  53.4 4.3 %all-to-all-done = f32[16,2,56,128]{3,2,1,0:T(8,128)S(1)} async-done(((f32[16,2,56,128]{3,2,1,0:T(8,128)}), f32[16,2,56,128]{3,2,1,0:T(8,128)S(1)}, u32[]{:S(2)}, u32[]{:S(2)}) %all-to-all-start) | async-done | bytes 917536 | tf_op jit(solution)/shard_map/all_to_all | solution.py:868
  57.7 0.0 copy-start
  57.7 1.1 %copy-done = bf16[768,512]{1,0:T(8,128)(2,1)S(1)} copy-done((bf16[768,512]{1,0:T(8,128)(2,1)S(1)}, bf16[768,512]{1,0:T(8,128)(2,1)}, u32[]{:S(2)}) %copy-start) | copy-done | bytes 786456
  58.8 6.5 %prolong.1 = f32[1,1,16,2,8,4096]{5,4,3,2,1,0:T(8,128)} custom-call(bf16[768,512]{1,0:T(8,128)(2,1)S(1)} %copy-done, f32[32,56,128]{2,1,0:T(8,128)S(1)} %bitcast.2), custom_call_target="tpu_custom_call" | custom-call | tf_op jit(solution)/shard_map/prolong/pallas_call | solution.py:837
Async XLA Ops:
  0.6 7.9 %copy-start.2 = (s32[16,1]{0,1:T(1,128)S(1)}, s32[16,1]{0,1:T(1,128)}, u32[]{:S(2)}) copy-start(s32[16,1]{0,1:T(1,128)} %param.6) | copy-start | bytes 196
  0.6 8.0 %copy-start.1 = (s32[2,2,32]{2,1,0:T(2,128)S(1)}, s32[2,2,32]{2,1,0:T(2,128)}, u32[]{:S(2)}) copy-start(s32[2,2,32]{2,1,0:T(2,128)} %flags.1) | copy-start | bytes 1540
  6.3 15.4 %collective-permute-start.2 = (f32[9,32,512]{2,1,0:T(8,128)}, f32[9,32,512]{2,1,0:T(8,128)S(1)}, u32[]{:S(2)}, u32[]{:S(2)}) collective-permute-start(f32[9,32,512]{2,1,0:T(8,128)} %get-tuple-element.17), channel_id=1, source_target_pairs={{0,1},{1,0},{2,3},{3,2},{4,5},{5,4},{6,7},{7,6},{8,9},{9,8},{10,11... | collective-permute-start | bytes 1769480 | tf_op jit(solution)/shard_map/ppermute | solution.py:857
  7.9 13.8 %collective-permute-start.3 = (f32[9,32,512]{2,1,0:T(8,128)}, f32[9,32,512]{2,1,0:T(8,128)S(1)}, u32[]{:S(2)}, u32[]{:S(2)}) collective-permute-start(f32[9,32,512]{2,1,0:T(8,128)} %get-tuple-element.18), channel_id=1, source_target_pairs={{1,2},{2,1},{3,4},{4,3},{5,6},{6,5},{7,8},{8,7},{9,10},{10,9},{11,... | collective-permute-start | bytes 1769480 | tf_op jit(solution)/shard_map/ppermute | solution.py:858
  16.6 7.7 %collective-permute-start = (f32[9,32,512]{2,1,0:T(8,128)S(1)}, f32[9,32,512]{2,1,0:T(8,128)S(1)}, u32[]{:S(2)}, u32[]{:S(2)}) collective-permute-start(f32[9,32,512]{2,1,0:T(8,128)S(1)} %get-tuple-element.15), channel_id=1, source_target_pairs={{0,16},{16,0},{32,48},{48,32},{64,80},{80,64},{96,112},{112,96},{1... | collective-permute-start | bytes 1769480 | tf_op jit(solution)/shard_map/ppermute | solution.py:860
  16.7 11.2 %collective-permute-start.1 = (f32[9,32,512]{2,1,0:T(8,128)S(1)}, f32[9,32,512]{2,1,0:T(8,128)S(1)}, u32[]{:S(2)}, u32[]{:S(2)}) collective-permute-start(f32[9,32,512]{2,1,0:T(8,128)S(1)} %get-tuple-element.16), channel_id=1, source_target_pairs={{16,32},{32,16},{48,64},{64,48},{80,96},{96,80},{17,33},{33,17},{4... | collective-permute-start | bytes 1769480 | tf_op jit(solution)/shard_map/ppermute | solution.py:861
  21.9 8.8 %collective-permute-start.4 = (f32[2,16,512]{2,1,0:T(8,128)S(1)}, f32[2,16,512]{2,1,0:T(8,128)S(1)}, u32[]{:S(2)}, u32[]{:S(2)}) collective-permute-start(f32[2,16,512]{2,1,0:T(8,128)S(1)} %get-tuple-element.21), channel_id=1, source_target_pairs={{0,16},{16,0},{32,48},{48,32},{64,80},{80,64},{96,112},{112,96},{1... | collective-permute-start | bytes 196616 | tf_op jit(solution)/shard_map/ppermute | solution.py:863
  22.0 8.7 %collective-permute-start.5 = (f32[2,16,512]{2,1,0:T(8,128)S(1)}, f32[2,16,512]{2,1,0:T(8,128)S(1)}, u32[]{:S(2)}, u32[]{:S(2)}) collective-permute-start(f32[2,16,512]{2,1,0:T(8,128)S(1)} %get-tuple-element.22), channel_id=1, source_target_pairs={{16,32},{32,16},{48,64},{64,48},{80,96},{96,80},{17,33},{33,17},{4... | collective-permute-start | bytes 196616 | tf_op jit(solution)/shard_map/ppermute | solution.py:864
  30.8 26.9 %all-to-all-start = ((f32[16,2,56,128]{3,2,1,0:T(8,128)}), f32[16,2,56,128]{3,2,1,0:T(8,128)S(1)}, u32[]{:S(2)}, u32[]{:S(2)}) async-start(f32[16,2,56,128]{3,2,1,0:T(8,128)} %bitcast), calls=%async_computation | async-start | bytes 1835008 | tf_op jit(solution)/shard_map/all_to_all | solution.py:868
  57.7 1.1 %copy-start = (bf16[768,512]{1,0:T(8,128)(2,1)S(1)}, bf16[768,512]{1,0:T(8,128)(2,1)}, u32[]{:S(2)}) copy-start(bf16[768,512]{1,0:T(8,128)(2,1)} %constant.2.clone.weights) | copy-start | bytes 2359300

commit v4 on v3

--- a/solution.py
+++ b/solution.py
@@ -256,17 +256,7 @@
         rolled = functools.cache(lambda k: pltpu.roll(value(k), 1, 1) if k >= 0 else zero)
         return lambda k: jnp.where(lane == 0, rolled(k - 1), rolled(k))
 
-    def plane(p, carry):
-        @pl.when((p % chunk == 0) & (p < nx))
-        def _():
-            for copy in chunk_in(p // chunk):
-                copy.wait()
-
-        @pl.when((p % chunk == 0) & (p < nx - ahead * chunk))
-        def _():
-            for copy in chunk_in(p // chunk + ahead):
-                copy.start()
-
+    def plane(p):
         at_rim = pl.ds(p + 7, 1)
         for k in range(nk):
             first = flds[4, p, 0:1, cut(k)]
@@ -324,12 +314,6 @@
                 prev[1, k, at] = z_sum
                 prev[2, k, at] = y_sum
 
-        @pl.when((p > chunk) & ((p - 1) % chunk == 0))
-        def _():
-            chunk_out((p - 1) // chunk - 1).start()
-
-        return carry
-
     def chunk_out(c):
         return pltpu.make_async_copy(
             done.at[:, pl.ds(1 + c * chunk, chunk)],
@@ -337,7 +321,28 @@
             out_sems.at[c],
         )
 
-    lax.fori_loop(0, nx + 2, plane, 0)
+    def step(c, carry):
+        for copy in chunk_in(c):
+            copy.wait()
+
+        @pl.when(c < chunks - ahead)
+        def _():
+            for copy in chunk_in(c + ahead):
+                copy.start()
+
+        for n in range(chunk):
+            plane(c * chunk + n)
+
+        @pl.when(c > 0)
+        def _():
+            chunk_out(c - 1).start()
+
+        return carry
+
+    lax.fori_loop(0, chunks, step, 0)
+    plane(nx)
+    plane(nx + 1)
+    chunk_out(chunks - 1).start()
     for c in range(chunks):
         chunk_out(c).wait()
 
@@ -757,16 +762,14 @@
 
 
 def spread_weights():
-    spread = np.zeros((3, LANES, 512), np.float32)
-    for half in range(2):
-        for y in range(BS):
-            for z in range(BS):
-                at = half * 64 + y // 2 * 8 + z // 2
-                to = half * 256 + y * BS + z
-                spread[0, at, to] = 1.0
-                spread[1, at, to] = 0.25 * (2 * (y % 2) - 1)
-                spread[2, at, to] = 0.25 * (2 * (z % 2) - 1)
-    return spread
+    spread = np.zeros((3, 64, 256), np.float32)
+    for y in range(BS):
+        for z in range(BS):
+            at = y // 2 * 8 + z // 2
+            spread[0, at, y * BS + z] = 1.0
+            spread[1, at, y * BS + z] = 0.25 * (2 * (y % 2) - 1)
+            spread[2, at, y * BS + z] = 0.25 * (2 * (z % 2) - 1)
+    return spread.reshape(192, 256)
 
 
 def limited(left, right):
@@ -778,7 +781,17 @@
     return top, (value - top.astype(F32)).astype(BF16)
 
 
-def prolong_kernel(weights, piece, out, staged):
+def prolong_kernel(blocks, piece, out, staged, weights):
+    @pl.when(pl.program_id(0) == 0)
+    def _():
+        weights[...] = jnp.zeros_like(weights)
+        for n, block in enumerate((0, 0, 1, 2, 1, 2)):
+            for half in range(2):
+                at = n * LANES + half * 64
+                weights[at : at + 64, 256 * half : 256 * half + 256] = blocks[
+                    64 * block : 64 * block + 64
+                ]
+
     count = piece.shape[0]
     sub = lax.broadcasted_iota(jnp.int32, (8, LANES), 0)
     lane = lax.broadcasted_iota(jnp.int32, (8, LANES), 1)
@@ -811,14 +824,14 @@
         staged[2, at] = slope_y
         staged[3, at] = slope_z
 
-    lax.fori_loop(0, count, slopes, 0)
+    lax.fori_loop(0, count, slopes, 0, unroll=True)
 
     def dot(parts, matrix):
         halves = [halves_of(staged[n]) for n in parts]
         value = jnp.concatenate([h[0] for h in halves] + [h[1] for h in halves], axis=1)
         return jnp.dot(value, matrix, preferred_element_type=F32)
 
-    tilt = dot((2, 3), weights[2 * LANES :])
+    tilt = dot((2, 3), weights[2 * LANES : 6 * LANES])
     for p in range(2):
         fine = dot((p,), weights[0 : 2 * LANES]) + tilt
         for s in range(count):
@@ -832,23 +845,25 @@
 
 def prolong(received, count):
     group = 8
-    weights = spread_weights()
-    stacked = np.concatenate([weights[n] for n in (0, 0, 1, 2, 1, 2)])
+    blocks = spread_weights()
     return pl.pallas_call(
         prolong_kernel,
         grid=(count * CAP // group,),
         out_shape=jax.ShapeDtypeStruct((1, 1, count, CAP, 8, BS**3), F32),
         in_specs=[
-            pl.BlockSpec(stacked.shape, lambda g: (0, 0)),
+            pl.BlockSpec(blocks.shape, lambda g: (0, 0)),
             pl.BlockSpec((group, ROWS, LANES), lambda g: (g, 0, 0)),
         ],
         out_specs=pl.BlockSpec(
             (1, 1, group // CAP, CAP, 8, BS**3), lambda g: (0, 0, g, 0, 0, 0)
         ),
-        scratch_shapes=[pltpu.VMEM((4, group * 32, LANES), F32)],
+        scratch_shapes=[
+            pltpu.VMEM((4, group * 32, LANES), F32),
+            pltpu.VMEM((6 * LANES, 512), BF16),
+        ],
         compiler_params=pltpu.CompilerParams(vmem_limit_bytes=16 * MIB),
         name="prolong",
-    )(jnp.asarray(stacked, BF16), received)
+    )(jnp.asarray(blocks, BF16), received)
 
 
 def on_device(state, flags, owners):

time: 65.6 us -> 62 us (0.945)
  Pallas kernels: 35.5 us -> 31 us
  waiting for transfers between devices: 10.4 us -> 12.5 us
  local copies, waits for them, and re-layouts: 1.23 us -> 0.1 us
    pallas_call x1, Pallas kernels: 6.46 us -> 4.01 us  [prolong(): pl.pallas_call(prolong_kernel, grid=(count * CAP // group,), out_shape=ja...]
    pallas_call x1, Pallas kernels: 12.3 us -> 10.3 us  [advance(): pl.pallas_call(advance_kernel, out_shape=jax.ShapeDtypeStruct((3, nx, ny,...]
    all_to_all x1, waiting for transfers between devices: 4.31 us -> 6.33 us  [on_device(): lax.all_to_all(sent.reshape((cols, CAP) + sent.shape[1:]), 'cols', split_...]
    unnamed x7, local copies, waits for them, and re-layouts: 1.23 us -> 0.1 us
  transfers between devices with their start and end apart: 7 -> 7, of which waited for: 3 -> 3; matrix products, arithmetic and copies ran while one was open for 0% -> 0% of each run, Pallas kernels for 36% -> 35%
where the time goes in v4:
time: 62 us; the launch traced here: 61.7 us
  Pallas kernels  31 us (50%)
  starting transfers between devices  17.3 us (28%)
  waiting for transfers between devices  12.5 us (20%)
  between operations  0.78 us (1%)
    pallas_call x1, Pallas kernels, advance(): pl.pallas_call(advance_kernel, out_shape=jax.ShapeDtypeStruct((3, nx, ny,...  10.3 us
    all_to_all x1, starting transfers between devices, on_device(): lax.all_to_all(sent.reshape((cols, CAP) + sent.shape[1:]), 'cols', split_...  10.2 us
    pallas_call x1, Pallas kernels, own_pieces(): pl.pallas_call(own_kernel, out_shape=[jax.ShapeDtypeStruct((KIDS, ROWS, L...  7.93 us
    all_to_all x1, waiting for transfers between devices, on_device(): lax.all_to_all(sent.reshape((cols, CAP) + sent.shape[1:]), 'cols', split_...  6.33 us
    pallas_call x1, Pallas kernels, pack(): pl.pallas_call(pack_kernel, out_shape=[col_shape, col_shape, jax.ShapeDty...  5.62 us
    pallas_call x1, Pallas kernels, prolong(): pl.pallas_call(prolong_kernel, grid=(count * CAP // group,), out_shape=ja...  4.01 us
    ppermute x1, waiting for transfers between devices, on_device(): row_odd = lax.ppermute(row_odd, 'rows', odd_swap(rows))  3.62 us
    pallas_call x1, Pallas kernels, finish_pieces(): pl.pallas_call(finish_kernel, out_shape=jax.ShapeDtypeStruct((count * CAP...  2.88 us
  transfers between devices with their start and end apart: 7, of which 3 were waited for; matrix products, arithmetic and copies ran while one was open for 0% of the time, Pallas kernels for 35%

profile of v4, /device:TPU:8, one launch (start us, length us, event | category | flops | bytes accessed | tf_op | source)
XLA Modules:
  0.0 61.7 jit_solution(4707483062484139746)
XLA Ops:
  0.6 0.0 copy-start.2
  0.6 0.0 copy-start.1
  0.6 5.6 %pack.1 = (f32[9,32,512]{2,1,0:T(8,128)}, f32[9,32,512]{2,1,0:T(8,128)}, s32[1]{0:T(128)}) custom-call(f32[8,32,32,512]{3,2,1,0:T(8,128)} %state.5), custom_call_target="tpu_custom_call" | custom-call | tf_op jit(solution)/shard_map/pack/pallas_call | solution.py:93
  6.3 1.6 %collective-permute-start.2 = (f32[9,32,512]{2,1,0:T(8,128)}, f32[9,32,512]{2,1,0:T(8,128)S(1)}, u32[]{:S(2)}, u32[]{:S(2)}) collective-permute-start(f32[9,32,512]{2,1,0:T(8,128)} %get-tuple-element.17), channel_id=1, source_target_pairs={{0,1},{1,0},{2,3},{3,2},{4,5},{5,4},{6,7},{7,6},{8,9},{9,8},{10,11... | collective-permute-start | bytes 1769480 | tf_op jit(solution)/shard_map/ppermute | solution.py:872
  7.9 0.7 %collective-permute-start.3 = (f32[9,32,512]{2,1,0:T(8,128)}, f32[9,32,512]{2,1,0:T(8,128)S(1)}, u32[]{:S(2)}, u32[]{:S(2)}) collective-permute-start(f32[9,32,512]{2,1,0:T(8,128)} %get-tuple-element.18), channel_id=1, source_target_pairs={{1,2},{2,1},{3,4},{4,3},{5,6},{6,5},{7,8},{8,7},{9,10},{10,9},{11,... | collective-permute-start | bytes 1769480 | tf_op jit(solution)/shard_map/ppermute | solution.py:873
  8.5 0.0 copy-done.2
  8.6 0.1 copy.6.owners
  8.6 0.0 copy-done.1
  8.6 7.9 %own_pieces.1 = (f32[16,56,128]{2,1,0:T(8,128)S(1)}, s32[22]{0:T(128)S(1)}, f32[9,32,512]{2,1,0:T(8,128)S(1)}, f32[9,32,512]{2,1,0:T(8,128)S(1)}) custom-call(s32[1]{0:T(128)} %get-tuple-element.14.token, f32[8,32,32,512]{3,2,1,0:T(8,128)} %state.5, s32[2,2,32]{2,1,0:T(2,128)S(1)} %copy-done.1, s32[16,1]{1,0:T(8,128)S(1)} %copy.6.owners), custom_call_target="tpu_custom_call" | custom-call | flops 10000000 | bytes 20000000 | tf_op jit(solution)/shard_map/own_pieces/pallas_call | solution.py:583
  16.6 0.1 collective-permute-start
  16.7 2.5 %collective-permute-start.1 = (f32[9,32,512]{2,1,0:T(8,128)S(1)}, f32[9,32,512]{2,1,0:T(8,128)S(1)}, u32[]{:S(2)}, u32[]{:S(2)}) collective-permute-start(f32[9,32,512]{2,1,0:T(8,128)S(1)} %get-tuple-element.16), channel_id=1, source_target_pairs={{16,32},{32,16},{48,64},{64,48},{80,96},{96,80},{17,33},{33,17},{4... | collective-permute-start | bytes 1769480 | tf_op jit(solution)/shard_map/ppermute | solution.py:876
  19.1 2.5 %collective-permute-done.2.col_even = f32[9,32,512]{2,1,0:T(8,128)S(1)} collective-permute-done((f32[9,32,512]{2,1,0:T(8,128)}, f32[9,32,512]{2,1,0:T(8,128)S(1)}, u32[]{:S(2)}, u32[]{:S(2)}) %collective-permute-start.2) | collective-permute-done | bytes 589856 | tf_op jit(solution)/shard_map/ppermute | solution.py:872
  21.6 0.0 collective-permute-done.3.col_odd
  21.6 0.3 pack_corners.1
  21.9 0.1 collective-permute-start.4
  22.0 2.2 %collective-permute-start.5 = (f32[2,16,512]{2,1,0:T(8,128)S(1)}, f32[2,16,512]{2,1,0:T(8,128)S(1)}, u32[]{:S(2)}, u32[]{:S(2)}) collective-permute-start(f32[2,16,512]{2,1,0:T(8,128)S(1)} %get-tuple-element.22), channel_id=1, source_target_pairs={{16,32},{32,16},{48,64},{64,48},{80,96},{96,80},{17,33},{33,17},{4... | collective-permute-start | bytes 196616 | tf_op jit(solution)/shard_map/ppermute | solution.py:879
  24.2 0.0 collective-permute-done.row_even
  24.3 3.6 %collective-permute-done.1.row_odd = f32[9,32,512]{2,1,0:T(8,128)S(1)} collective-permute-done((f32[9,32,512]{2,1,0:T(8,128)S(1)}, f32[9,32,512]{2,1,0:T(8,128)S(1)}, u32[]{:S(2)}, u32[]{:S(2)}) %collective-permute-start.1) | collective-permute-done | bytes 589856 | tf_op jit(solution)/shard_map/ppermute | solution.py:876
  27.9 2.9 %finish_pieces.1 = f32[32,56,128]{2,1,0:T(8,128)} custom-call(s32[22]{0:T(128)S(1)} %get-tuple-element.19.info, f32[16,56,128]{2,1,0:T(8,128)S(1)} %get-tuple-element.20.own, f32[9,32,512]{2,1,0:T(8,128)S(1)} %collective-permute-done.row_even, f32[9,32,512]{2,1,0:T(8,128)S(1)} %collective-permute-done.1.row_odd, ...), custom_call_target="tpu_custom_call" | custom-call | tf_op jit(solution)/shard_map/finish_pieces/pallas_call | solution.py:748
  30.8 0.0 collective-permute-done.4.cor_even
  30.8 0.0 collective-permute-done.5.cor_odd
  30.8 10.2 %all-to-all-start = ((f32[16,2,56,128]{3,2,1,0:T(8,128)}), f32[16,2,56,128]{3,2,1,0:T(8,128)S(1)}, u32[]{:S(2)}, u32[]{:S(2)}) async-start(f32[16,2,56,128]{3,2,1,0:T(8,128)} %bitcast), calls=%async_computation | async-start | bytes 1835008 | tf_op jit(solution)/shard_map/all_to_all | solution.py:883
  41.0 0.0 copy-start
  41.0 10.3 %advance.1 = f32[3,32,32,512]{3,2,1,0:T(8,128)} custom-call(f32[8,32,32,512]{3,2,1,0:T(8,128)} %state.5, f32[9,32,512]{2,1,0:T(8,128)S(1)} %collective-permute-done.row_even, f32[9,32,512]{2,1,0:T(8,128)S(1)} %collective-permute-done.1.row_odd, f32[9,32,512]{2,1,0:T(8,128)S(1)} %collective-permute-done.2.col_even, ...), custom_call_target="tpu_custom_call" | custom-call | flops 31457280 | bytes 20971520 | tf_op jit(solution)/shard_map/advance/pallas_call | solution.py:353
  51.3 6.3 %all-to-all-done = f32[16,2,56,128]{3,2,1,0:T(8,128)S(1)} async-done(((f32[16,2,56,128]{3,2,1,0:T(8,128)}), f32[16,2,56,128]{3,2,1,0:T(8,128)S(1)}, u32[]{:S(2)}, u32[]{:S(2)}) %all-to-all-start) | async-done | bytes 917536 | tf_op jit(solution)/shard_map/all_to_all | solution.py:883
  57.7 0.0 copy-done
  57.7 4.0 %prolong.1 = f32[1,1,16,2,8,4096]{5,4,3,2,1,0:T(8,128)} custom-call(bf16[192,256]{1,0:T(8,128)(2,1)S(1)} %copy-done, f32[32,56,128]{2,1,0:T(8,128)S(1)} %bitcast.2), custom_call_target="tpu_custom_call" | custom-call | tf_op jit(solution)/shard_map/prolong/pallas_call | solution.py:849
Async XLA Ops:
  0.6 7.9 %copy-start.2 = (s32[16,1]{0,1:T(1,128)S(1)}, s32[16,1]{0,1:T(1,128)}, u32[]{:S(2)}) copy-start(s32[16,1]{0,1:T(1,128)} %param.6) | copy-start | bytes 196
  0.6 8.0 %copy-start.1 = (s32[2,2,32]{2,1,0:T(2,128)S(1)}, s32[2,2,32]{2,1,0:T(2,128)}, u32[]{:S(2)}) copy-start(s32[2,2,32]{2,1,0:T(2,128)} %flags.1) | copy-start | bytes 1540
  6.3 15.4 %collective-permute-start.2 = (f32[9,32,512]{2,1,0:T(8,128)}, f32[9,32,512]{2,1,0:T(8,128)S(1)}, u32[]{:S(2)}, u32[]{:S(2)}) collective-permute-start(f32[9,32,512]{2,1,0:T(8,128)} %get-tuple-element.17), channel_id=1, source_target_pairs={{0,1},{1,0},{2,3},{3,2},{4,5},{5,4},{6,7},{7,6},{8,9},{9,8},{10,11... | collective-permute-start | bytes 1769480 | tf_op jit(solution)/shard_map/ppermute | solution.py:872
  7.9 13.8 %collective-permute-start.3 = (f32[9,32,512]{2,1,0:T(8,128)}, f32[9,32,512]{2,1,0:T(8,128)S(1)}, u32[]{:S(2)}, u32[]{:S(2)}) collective-permute-start(f32[9,32,512]{2,1,0:T(8,128)} %get-tuple-element.18), channel_id=1, source_target_pairs={{1,2},{2,1},{3,4},{4,3},{5,6},{6,5},{7,8},{8,7},{9,10},{10,9},{11,... | collective-permute-start | bytes 1769480 | tf_op jit(solution)/shard_map/ppermute | solution.py:873
  16.6 7.7 %collective-permute-start = (f32[9,32,512]{2,1,0:T(8,128)S(1)}, f32[9,32,512]{2,1,0:T(8,128)S(1)}, u32[]{:S(2)}, u32[]{:S(2)}) collective-permute-start(f32[9,32,512]{2,1,0:T(8,128)S(1)} %get-tuple-element.15), channel_id=1, source_target_pairs={{0,16},{16,0},{32,48},{48,32},{64,80},{80,64},{96,112},{112,96},{1... | collective-permute-start | bytes 1769480 | tf_op jit(solution)/shard_map/ppermute | solution.py:875
  16.7 11.2 %collective-permute-start.1 = (f32[9,32,512]{2,1,0:T(8,128)S(1)}, f32[9,32,512]{2,1,0:T(8,128)S(1)}, u32[]{:S(2)}, u32[]{:S(2)}) collective-permute-start(f32[9,32,512]{2,1,0:T(8,128)S(1)} %get-tuple-element.16), channel_id=1, source_target_pairs={{16,32},{32,16},{48,64},{64,48},{80,96},{96,80},{17,33},{33,17},{4... | collective-permute-start | bytes 1769480 | tf_op jit(solution)/shard_map/ppermute | solution.py:876
  21.9 8.8 %collective-permute-start.4 = (f32[2,16,512]{2,1,0:T(8,128)S(1)}, f32[2,16,512]{2,1,0:T(8,128)S(1)}, u32[]{:S(2)}, u32[]{:S(2)}) collective-permute-start(f32[2,16,512]{2,1,0:T(8,128)S(1)} %get-tuple-element.21), channel_id=1, source_target_pairs={{0,16},{16,0},{32,48},{48,32},{64,80},{80,64},{96,112},{112,96},{1... | collective-permute-start | bytes 196616 | tf_op jit(solution)/shard_map/ppermute | solution.py:878
  22.0 8.7 %collective-permute-start.5 = (f32[2,16,512]{2,1,0:T(8,128)S(1)}, f32[2,16,512]{2,1,0:T(8,128)S(1)}, u32[]{:S(2)}, u32[]{:S(2)}) collective-permute-start(f32[2,16,512]{2,1,0:T(8,128)S(1)} %get-tuple-element.22), channel_id=1, source_target_pairs={{16,32},{32,16},{48,64},{64,48},{80,96},{96,80},{17,33},{33,17},{4... | collective-permute-start | bytes 196616 | tf_op jit(solution)/shard_map/ppermute | solution.py:879
  30.8 26.9 %all-to-all-start = ((f32[16,2,56,128]{3,2,1,0:T(8,128)}), f32[16,2,56,128]{3,2,1,0:T(8,128)S(1)}, u32[]{:S(2)}, u32[]{:S(2)}) async-start(f32[16,2,56,128]{3,2,1,0:T(8,128)} %bitcast), calls=%async_computation | async-start | bytes 1835008 | tf_op jit(solution)/shard_map/all_to_all | solution.py:883
  41.0 16.7 %copy-start = (bf16[192,256]{1,0:T(8,128)(2,1)S(1)}, bf16[192,256]{1,0:T(8,128)(2,1)}, u32[]{:S(2)}) copy-start(bf16[192,256]{1,0:T(8,128)(2,1)} %constant.2.clone.blocks) | copy-start | bytes 294916

commit v5 on v4

--- a/solution.py
+++ b/solution.py
@@ -844,7 +844,7 @@
 
 
 def prolong(received, count):
-    group = 8
+    group = 16
     blocks = spread_weights()
     return pl.pallas_call(
         prolong_kernel,

time: 62 us -> 61.6 us (level)
  no operation moved by 1% of the time
where the time goes in v5:
time: 61.6 us; the launch traced here: 61.3 us
  Pallas kernels  30.7 us (50%)
  starting transfers between devices  17.3 us (28%)
  waiting for transfers between devices  12.5 us (20%)
  between operations  0.78 us (1%)
    pallas_call x1, Pallas kernels, advance(): pl.pallas_call(advance_kernel, out_shape=jax.ShapeDtypeStruct((3, nx, ny,...  10.3 us
    all_to_all x1, starting transfers between devices, on_device(): lax.all_to_all(sent.reshape((cols, CAP) + sent.shape[1:]), 'cols', split_...  10.2 us
    pallas_call x1, Pallas kernels, own_pieces(): pl.pallas_call(own_kernel, out_shape=[jax.ShapeDtypeStruct((KIDS, ROWS, L...  7.93 us
    all_to_all x1, waiting for transfers between devices, on_device(): lax.all_to_all(sent.reshape((cols, CAP) + sent.shape[1:]), 'cols', split_...  6.33 us
    pallas_call x1, Pallas kernels, pack(): pl.pallas_call(pack_kernel, out_shape=[col_shape, col_shape, jax.ShapeDty...  5.62 us
    ppermute x1, waiting for transfers between devices, on_device(): row_odd = lax.ppermute(row_odd, 'rows', odd_swap(rows))  3.62 us
    pallas_call x1, Pallas kernels, prolong(): pl.pallas_call(prolong_kernel, grid=(count * CAP // group,), out_shape=ja...  3.62 us
    pallas_call x1, Pallas kernels, finish_pieces(): pl.pallas_call(finish_kernel, out_shape=jax.ShapeDtypeStruct((count * CAP...  2.88 us
  transfers between devices with their start and end apart: 7, of which 3 were waited for; matrix products, arithmetic and copies ran while one was open for 0% of the time, Pallas kernels for 35%

profile of v5, /device:TPU:8, one launch (start us, length us, event | category | flops | bytes accessed | tf_op | source)
XLA Modules:
  0.0 61.3 jit_solution(10002657499949318585)
XLA Ops:
  0.6 0.0 copy-start.2
  0.6 0.0 copy-start.1
  0.6 5.6 %pack.1 = (f32[9,32,512]{2,1,0:T(8,128)}, f32[9,32,512]{2,1,0:T(8,128)}, s32[1]{0:T(128)}) custom-call(f32[8,32,32,512]{3,2,1,0:T(8,128)} %state.5), custom_call_target="tpu_custom_call" | custom-call | tf_op jit(solution)/shard_map/pack/pallas_call | solution.py:93
  6.3 1.6 %collective-permute-start.2 = (f32[9,32,512]{2,1,0:T(8,128)}, f32[9,32,512]{2,1,0:T(8,128)S(1)}, u32[]{:S(2)}, u32[]{:S(2)}) collective-permute-start(f32[9,32,512]{2,1,0:T(8,128)} %get-tuple-element.17), channel_id=1, source_target_pairs={{0,1},{1,0},{2,3},{3,2},{4,5},{5,4},{6,7},{7,6},{8,9},{9,8},{10,11... | collective-permute-start | bytes 1769480 | tf_op jit(solution)/shard_map/ppermute | solution.py:872
  7.9 0.7 %collective-permute-start.3 = (f32[9,32,512]{2,1,0:T(8,128)}, f32[9,32,512]{2,1,0:T(8,128)S(1)}, u32[]{:S(2)}, u32[]{:S(2)}) collective-permute-start(f32[9,32,512]{2,1,0:T(8,128)} %get-tuple-element.18), channel_id=1, source_target_pairs={{1,2},{2,1},{3,4},{4,3},{5,6},{6,5},{7,8},{8,7},{9,10},{10,9},{11,... | collective-permute-start | bytes 1769480 | tf_op jit(solution)/shard_map/ppermute | solution.py:873
  8.5 0.0 copy-done.2
  8.6 0.1 copy.6.owners
  8.6 0.0 copy-done.1
  8.6 7.9 %own_pieces.1 = (f32[16,56,128]{2,1,0:T(8,128)S(1)}, s32[22]{0:T(128)S(1)}, f32[9,32,512]{2,1,0:T(8,128)S(1)}, f32[9,32,512]{2,1,0:T(8,128)S(1)}) custom-call(s32[1]{0:T(128)} %get-tuple-element.14.token, f32[8,32,32,512]{3,2,1,0:T(8,128)} %state.5, s32[2,2,32]{2,1,0:T(2,128)S(1)} %copy-done.1, s32[16,1]{1,0:T(8,128)S(1)} %copy.6.owners), custom_call_target="tpu_custom_call" | custom-call | flops 10000000 | bytes 20000000 | tf_op jit(solution)/shard_map/own_pieces/pallas_call | solution.py:583
  16.6 0.1 collective-permute-start
  16.7 2.4 %collective-permute-start.1 = (f32[9,32,512]{2,1,0:T(8,128)S(1)}, f32[9,32,512]{2,1,0:T(8,128)S(1)}, u32[]{:S(2)}, u32[]{:S(2)}) collective-permute-start(f32[9,32,512]{2,1,0:T(8,128)S(1)} %get-tuple-element.16), channel_id=1, source_target_pairs={{16,32},{32,16},{48,64},{64,48},{80,96},{96,80},{17,33},{33,17},{4... | collective-permute-start | bytes 1769480 | tf_op jit(solution)/shard_map/ppermute | solution.py:876
  19.1 2.5 %collective-permute-done.2.col_even = f32[9,32,512]{2,1,0:T(8,128)S(1)} collective-permute-done((f32[9,32,512]{2,1,0:T(8,128)}, f32[9,32,512]{2,1,0:T(8,128)S(1)}, u32[]{:S(2)}, u32[]{:S(2)}) %collective-permute-start.2) | collective-permute-done | bytes 589856 | tf_op jit(solution)/shard_map/ppermute | solution.py:872
  21.6 0.0 collective-permute-done.3.col_odd
  21.6 0.3 pack_corners.1
  21.9 0.1 collective-permute-start.4
  22.0 2.2 %collective-permute-start.5 = (f32[2,16,512]{2,1,0:T(8,128)S(1)}, f32[2,16,512]{2,1,0:T(8,128)S(1)}, u32[]{:S(2)}, u32[]{:S(2)}) collective-permute-start(f32[2,16,512]{2,1,0:T(8,128)S(1)} %get-tuple-element.22), channel_id=1, source_target_pairs={{16,32},{32,16},{48,64},{64,48},{80,96},{96,80},{17,33},{33,17},{4... | collective-permute-start | bytes 196616 | tf_op jit(solution)/shard_map/ppermute | solution.py:879
  24.2 0.0 collective-permute-done.row_even
  24.3 3.6 %collective-permute-done.1.row_odd = f32[9,32,512]{2,1,0:T(8,128)S(1)} collective-permute-done((f32[9,32,512]{2,1,0:T(8,128)S(1)}, f32[9,32,512]{2,1,0:T(8,128)S(1)}, u32[]{:S(2)}, u32[]{:S(2)}) %collective-permute-start.1) | collective-permute-done | bytes 589856 | tf_op jit(solution)/shard_map/ppermute | solution.py:876
  27.9 2.9 %finish_pieces.1 = f32[32,56,128]{2,1,0:T(8,128)} custom-call(s32[22]{0:T(128)S(1)} %get-tuple-element.19.info, f32[16,56,128]{2,1,0:T(8,128)S(1)} %get-tuple-element.20.own, f32[9,32,512]{2,1,0:T(8,128)S(1)} %collective-permute-done.row_even, f32[9,32,512]{2,1,0:T(8,128)S(1)} %collective-permute-done.1.row_odd, ...), custom_call_target="tpu_custom_call" | custom-call | tf_op jit(solution)/shard_map/finish_pieces/pallas_call | solution.py:748
  30.8 0.0 collective-permute-done.4.cor_even
  30.8 0.0 collective-permute-done.5.cor_odd
  30.8 10.2 %all-to-all-start = ((f32[16,2,56,128]{3,2,1,0:T(8,128)}), f32[16,2,56,128]{3,2,1,0:T(8,128)S(1)}, u32[]{:S(2)}, u32[]{:S(2)}) async-start(f32[16,2,56,128]{3,2,1,0:T(8,128)} %bitcast), calls=%async_computation | async-start | bytes 1835008 | tf_op jit(solution)/shard_map/all_to_all | solution.py:883
  41.0 0.0 copy-start
  41.0 10.3 %advance.1 = f32[3,32,32,512]{3,2,1,0:T(8,128)} custom-call(f32[8,32,32,512]{3,2,1,0:T(8,128)} %state.5, f32[9,32,512]{2,1,0:T(8,128)S(1)} %collective-permute-done.row_even, f32[9,32,512]{2,1,0:T(8,128)S(1)} %collective-permute-done.1.row_odd, f32[9,32,512]{2,1,0:T(8,128)S(1)} %collective-permute-done.2.col_even, ...), custom_call_target="tpu_custom_call" | custom-call | flops 31457280 | bytes 20971520 | tf_op jit(solution)/shard_map/advance/pallas_call | solution.py:353
  51.3 6.3 %all-to-all-done = f32[16,2,56,128]{3,2,1,0:T(8,128)S(1)} async-done(((f32[16,2,56,128]{3,2,1,0:T(8,128)}), f32[16,2,56,128]{3,2,1,0:T(8,128)S(1)}, u32[]{:S(2)}, u32[]{:S(2)}) %all-to-all-start) | async-done | bytes 917536 | tf_op jit(solution)/shard_map/all_to_all | solution.py:883
  57.7 0.0 copy-done
  57.7 3.6 %prolong.1 = f32[1,1,16,2,8,4096]{5,4,3,2,1,0:T(8,128)} custom-call(bf16[192,256]{1,0:T(8,128)(2,1)S(1)} %copy-done, f32[32,56,128]{2,1,0:T(8,128)S(1)} %bitcast.2), custom_call_target="tpu_custom_call" | custom-call | tf_op jit(solution)/shard_map/prolong/pallas_call | solution.py:849
Async XLA Ops:
  0.6 7.9 %copy-start.2 = (s32[16,1]{0,1:T(1,128)S(1)}, s32[16,1]{0,1:T(1,128)}, u32[]{:S(2)}) copy-start(s32[16,1]{0,1:T(1,128)} %param.6) | copy-start | bytes 196
  0.6 8.0 %copy-start.1 = (s32[2,2,32]{2,1,0:T(2,128)S(1)}, s32[2,2,32]{2,1,0:T(2,128)}, u32[]{:S(2)}) copy-start(s32[2,2,32]{2,1,0:T(2,128)} %flags.1) | copy-start | bytes 1540
  6.3 15.4 %collective-permute-start.2 = (f32[9,32,512]{2,1,0:T(8,128)}, f32[9,32,512]{2,1,0:T(8,128)S(1)}, u32[]{:S(2)}, u32[]{:S(2)}) collective-permute-start(f32[9,32,512]{2,1,0:T(8,128)} %get-tuple-element.17), channel_id=1, source_target_pairs={{0,1},{1,0},{2,3},{3,2},{4,5},{5,4},{6,7},{7,6},{8,9},{9,8},{10,11... | collective-permute-start | bytes 1769480 | tf_op jit(solution)/shard_map/ppermute | solution.py:872
  7.9 13.8 %collective-permute-start.3 = (f32[9,32,512]{2,1,0:T(8,128)}, f32[9,32,512]{2,1,0:T(8,128)S(1)}, u32[]{:S(2)}, u32[]{:S(2)}) collective-permute-start(f32[9,32,512]{2,1,0:T(8,128)} %get-tuple-element.18), channel_id=1, source_target_pairs={{1,2},{2,1},{3,4},{4,3},{5,6},{6,5},{7,8},{8,7},{9,10},{10,9},{11,... | collective-permute-start | bytes 1769480 | tf_op jit(solution)/shard_map/ppermute | solution.py:873
  16.6 7.7 %collective-permute-start = (f32[9,32,512]{2,1,0:T(8,128)S(1)}, f32[9,32,512]{2,1,0:T(8,128)S(1)}, u32[]{:S(2)}, u32[]{:S(2)}) collective-permute-start(f32[9,32,512]{2,1,0:T(8,128)S(1)} %get-tuple-element.15), channel_id=1, source_target_pairs={{0,16},{16,0},{32,48},{48,32},{64,80},{80,64},{96,112},{112,96},{1... | collective-permute-start | bytes 1769480 | tf_op jit(solution)/shard_map/ppermute | solution.py:875
  16.7 11.2 %collective-permute-start.1 = (f32[9,32,512]{2,1,0:T(8,128)S(1)}, f32[9,32,512]{2,1,0:T(8,128)S(1)}, u32[]{:S(2)}, u32[]{:S(2)}) collective-permute-start(f32[9,32,512]{2,1,0:T(8,128)S(1)} %get-tuple-element.16), channel_id=1, source_target_pairs={{16,32},{32,16},{48,64},{64,48},{80,96},{96,80},{17,33},{33,17},{4... | collective-permute-start | bytes 1769480 | tf_op jit(solution)/shard_map/ppermute | solution.py:876
  21.9 8.8 %collective-permute-start.4 = (f32[2,16,512]{2,1,0:T(8,128)S(1)}, f32[2,16,512]{2,1,0:T(8,128)S(1)}, u32[]{:S(2)}, u32[]{:S(2)}) collective-permute-start(f32[2,16,512]{2,1,0:T(8,128)S(1)} %get-tuple-element.21), channel_id=1, source_target_pairs={{0,16},{16,0},{32,48},{48,32},{64,80},{80,64},{96,112},{112,96},{1... | collective-permute-start | bytes 196616 | tf_op jit(solution)/shard_map/ppermute | solution.py:878
  22.0 8.7 %collective-permute-start.5 = (f32[2,16,512]{2,1,0:T(8,128)S(1)}, f32[2,16,512]{2,1,0:T(8,128)S(1)}, u32[]{:S(2)}, u32[]{:S(2)}) collective-permute-start(f32[2,16,512]{2,1,0:T(8,128)S(1)} %get-tuple-element.22), channel_id=1, source_target_pairs={{16,32},{32,16},{48,64},{64,48},{80,96},{96,80},{17,33},{33,17},{4... | collective-permute-start | bytes 196616 | tf_op jit(solution)/shard_map/ppermute | solution.py:879
  30.8 26.9 %all-to-all-start = ((f32[16,2,56,128]{3,2,1,0:T(8,128)}), f32[16,2,56,128]{3,2,1,0:T(8,128)S(1)}, u32[]{:S(2)}, u32[]{:S(2)}) async-start(f32[16,2,56,128]{3,2,1,0:T(8,128)} %bitcast), calls=%async_computation | async-start | bytes 1835008 | tf_op jit(solution)/shard_map/all_to_all | solution.py:883
  41.0 16.7 %copy-start = (bf16[192,256]{1,0:T(8,128)(2,1)S(1)}, bf16[192,256]{1,0:T(8,128)(2,1)}, u32[]{:S(2)}) copy-start(bf16[192,256]{1,0:T(8,128)(2,1)} %constant.2.clone.blocks) | copy-start | bytes 294916
